TPU v7x, 256 devices: a whole 4x4x8 slice. The times are simulated.
256 devices in a mesh: seq: 128 (over x, y, z), head: 2 (over core).
Axes of the slice: x: 4, y: 4, z: 8, core: 2. Of those that a mesh axis runs over, the one named last changes fastest.
Arguments:
- queries: bfloat16 [16384, 2048], P('seq', 'head'), may hold values from -0.52734375 to 0.52734375
- keys: bfloat16 [16384, 2048], P('seq', 'head'), may hold values from -0.52734375 to 0.52734375
- values: bfloat16 [16384, 2048], P('seq', 'head'), may hold values from -6 to 6
- transitions: bfloat16 [256, 16, 128, 128], P('seq', 'head'), may hold values from -0.03 to 1, as said below
- gates: float32 [256, 16], P('seq', 'head'), may hold values from 0.02 to 1
- norm_gain: float32 [128], replicated, may hold values from 0.25 to 1.75
Outputs:
- output: bfloat16 [16384, 2048], P(('seq', 'head'))
Inputs may be any that keep to these rules, and one draw needn't show every extreme that they name: `transitions`: diagonal entries lie between 0.99 and 1; off-diagonal entries are small.
All inputs are finite; a program needn't handle non-finite values.
Results may differ from a plain program's by a relative error of at most 0.0095.
Values may be sent and summed in bfloat16 or wider, within the bound.
No kernel may reach another device: no remote copies, remote signals or barrier semaphores. Data moves between devices by JAX's collectives and lax.ppermute only.
A program may use at most 256 MiB of HBM per device.

v0:
```python
import jax
import jax.numpy as jnp
from jax import lax
from jax.sharding import PartitionSpec as P

EPS = 1e-06


def matmul_batch(left, right):
    return jnp.einsum("hij,hjk->hik", left, right, precision=lax.Precision.HIGHEST)


def shards(queries, keys, values, transitions, gates, norm_gain):
    local_segments = transitions.shape[0]
    heads_here = transitions.shape[1]
    key_width = transitions.shape[2]
    value_width = values.shape[1] // heads_here
    tok_rows = queries.shape[0]
    block_len = tok_rows // local_segments
    query_r = queries.reshape(local_segments, block_len, heads_here, key_width)
    key_r = keys.reshape(local_segments, block_len, heads_here, key_width)
    value_r = values.reshape(local_segments, block_len, heads_here, value_width)
    transit = transitions.astype(jnp.float32) * gates[:, :, None, None]
    updates = jnp.einsum("cthd,cthe->chde", key_r, value_r, preferred_element_type=jnp.float32)
    identity_maps = jnp.broadcast_to(
        jnp.eye(key_width, dtype=jnp.float32), (heads_here, key_width, key_width)
    )
    zero_state = jnp.zeros((heads_here, key_width, value_width), jnp.float32)

    def compose(totals, inputs):
        map_total, upd_total = totals
        full_map, update = inputs
        return (
            (matmul_batch(full_map, map_total), matmul_batch(full_map, upd_total) + update),
            None,
        )

    (map_total, upd_total), _ = lax.scan(compose, (identity_maps, zero_state), (transit, updates))
    device_count = lax.axis_size("seq")
    owners = device_count // heads_here
    col_width = value_width // owners
    send_upd = (
        upd_total.reshape(heads_here, key_width, owners, col_width)
        .transpose(0, 2, 3, 1)
        .reshape(device_count, col_width, key_width)
    )
    outgoing_map = jnp.broadcast_to(
        map_total[:, None], (heads_here, owners, key_width, key_width)
    ).reshape(device_count, key_width, key_width)
    got_map, got_upd = (
        lax.all_to_all(outgoing_map, "seq", split_axis=0, concat_axis=0, tiled=True),
        lax.all_to_all(send_upd, "seq", split_axis=0, concat_axis=0, tiled=True),
    )

    def relay(owner_state, inputs):
        source_map, source_upd = inputs
        following = (
            lax.dot_general(
                owner_state, source_map, (((1,), (1,)), ((), ())), precision=lax.Precision.HIGHEST
            )
            + source_upd
        )
        return (following, owner_state)

    _, prefix = lax.scan(relay, jnp.zeros((col_width, key_width), jnp.float32), (got_map, got_upd))
    returned = lax.all_to_all(prefix, "seq", split_axis=0, concat_axis=0, tiled=True)
    entering = (
        returned.reshape(heads_here, owners, col_width, key_width)
        .transpose(0, 3, 1, 2)
        .reshape(heads_here, key_width, value_width)
    )

    def advance(carry_state, inputs):
        full_map, update = inputs
        return (matmul_batch(full_map, carry_state) + update, carry_state)

    _, states = lax.scan(advance, entering, (transit, updates))
    state_rounded = states.astype(jnp.bfloat16)
    carried = jnp.einsum(
        "cthd,chde->cthe", query_r, state_rounded, preferred_element_type=jnp.float32
    )
    scores = jnp.einsum("cthd,cshd->chts", query_r, key_r, preferred_element_type=jnp.float32)
    causal = jnp.tril(jnp.ones((block_len, block_len), dtype=bool))
    weights = jnp.where(causal[None, None], scores, 0.0).astype(jnp.bfloat16)
    local_term = jnp.einsum("chts,cshe->cthe", weights, value_r, preferred_element_type=jnp.float32)
    mixed = carried + local_term
    factor = lax.rsqrt(jnp.mean(mixed * mixed, axis=-1, keepdims=True) + EPS)
    normed = (
        (mixed * factor * norm_gain)
        .astype(jnp.bfloat16)
        .reshape(tok_rows, heads_here * value_width)
    )
    return lax.all_to_all(normed, "head", split_axis=0, concat_axis=1, tiled=True)


def solution(mesh):
    placed = (
        P("seq", "head"),
        P("seq", "head"),
        P("seq", "head"),
        P("seq", "head", None, None),
        P("seq", "head"),
        P(),
    )
    return jax.shard_map(
        shards, mesh=mesh, in_specs=placed, out_specs=P(("seq", "head"), None), check_vma=False
    )
```

profile of v0, /device:TPU:1, one launch (start us, length us, event | category | flops | bytes accessed | tf_op | source)
XLA Modules:
  0.0 492.1 jit_solution(16513995016824292156)
XLA Ops:
  3.1 1.2 convert_multiply_fusion
  4.3 2.9 while.39
  8.2 35.4 %all_to_all.34 = f32[128,8,128]{2,1,0:T(8,128)S(1)} all-to-all(f32[128,8,128]{2,1,0:T(8,128)} %bitcast.94), channel_id=1, replica_groups=mesh['seq'=128,'head'=2] {'seq'}, dimensions={0} | all-to-all | bytes 1048576 | tf_op jit(solution)/shard_map/all_to_all | solution.py:52
  43.6 4.3 broadcast_in_dim.52
  47.9 7.6 %all-to-all-start = ((f32[128,128,128]{2,1,0:T(8,128)}), f32[128,128,128]{2,1,0:T(8,128)}, u32[]{:S(2)}, u32[]{:S(2)}) async-start(f32[128,128,128]{2,1,0:T(8,128)} %bitcast.86), calls=%async_computation | async-start | bytes 16777216 | tf_op jit(solution)/shard_map/all_to_all | solution.py:51
  55.6 183.2 %all-to-all-done = f32[128,128,128]{2,1,0:T(8,128)} async-done(((f32[128,128,128]{2,1,0:T(8,128)}), f32[128,128,128]{2,1,0:T(8,128)}, u32[]{:S(2)}, u32[]{:S(2)}) %all-to-all-start) | async-done | bytes 8388640 | tf_op jit(solution)/shard_map/all_to_all | solution.py:51
  238.8 212.8 %while.40 = (s32[]{:T(128)}, f32[8,128]{1,0:T(8,128)S(1)}, f32[128,8,128]{2,1,0:T(8,128)}, f32[128,128,128]{2,1,0:T(8,128)}, f32[128,8,128]{2,1,0:T(8,128)S(1)}, /*index=5*/s32[]{:T(128)}, s32[]{:T(128)}) while((s32[]{:T(128)}, f32[8,128]{1,0:T(8,128)S(1)}, f32[128,8,128]{2,1,0:T(8,128)}, f32[128,128,128]{2,1,0:T(8,128)}, ...), condition=%wide.region_3.4_spmd.clone, body=%wide.region_2.3_spmd.clone.sunk | while | flops 1575939 | bytes 95832 | solution.py:65
  239.4 1.0 fusion.66
  241.1 1.0 fusion.66
  242.7 1.0 fusion.66
  244.4 1.0 fusion.66
  246.0 1.0 fusion.66
  247.7 1.0 fusion.66
  249.4 1.0 fusion.66
  251.0 1.0 fusion.66
  252.7 1.0 fusion.66
  254.4 1.0 fusion.66
  256.0 1.0 fusion.66
  257.7 1.0 fusion.66
  259.4 1.0 fusion.66
  261.0 1.0 fusion.66
  262.7 1.0 fusion.66
  264.3 1.0 fusion.66
  266.0 1.0 fusion.66
  267.7 1.0 fusion.66
  269.3 1.0 fusion.66
  271.0 1.0 fusion.66
  272.7 1.0 fusion.66
  274.3 1.0 fusion.66
  276.0 1.0 fusion.66
  277.7 1.0 fusion.66
  279.3 1.0 fusion.66
  281.0 1.0 fusion.66
  282.6 1.0 fusion.66
  294.3 1.0 fusion.66
  305.9 1.0 fusion.66
  315.9 1.0 fusion.66
  317.6 1.0 fusion.66
  324.2 1.0 fusion.66
  347.5 1.0 fusion.66
  354.2 1.0 fusion.66
  355.8 1.0 fusion.66
  357.5 1.0 fusion.66
  362.5 1.0 fusion.66
  364.1 1.0 fusion.66
  367.5 1.0 fusion.66
  374.1 1.0 fusion.66
  380.7 1.0 fusion.66
  384.1 1.0 fusion.66
  387.4 1.0 fusion.66
  395.7 1.0 fusion.66
  410.7 1.0 fusion.66
  419.0 1.0 fusion.66
  425.6 1.0 fusion.66
  430.6 1.0 fusion.66
  432.3 1.0 fusion.66
  435.6 1.0 fusion.66
  445.5 1.0 fusion.66
  451.5 7.6 %all-to-all-start.2 = ((f32[128,8,128]{2,1,0:T(8,128)}), f32[128,8,128]{2,1,0:T(8,128)S(1)}, u32[]{:S(2)}, u32[]{:S(2)}) async-start(f32[128,8,128]{2,1,0:T(8,128)} %get-tuple-element.89), calls=%async_computation.2 | async-start | bytes 1048576 | tf_op jit(solution)/shard_map/all_to_all | solution.py:66
  459.2 16.1 %all-to-all-done.2 = f32[128,8,128]{2,1,0:T(8,128)S(1)} async-done(((f32[128,8,128]{2,1,0:T(8,128)}), f32[128,8,128]{2,1,0:T(8,128)S(1)}, u32[]{:S(2)}, u32[]{:S(2)}) %all-to-all-start.2) | async-done | bytes 524320 | tf_op jit(solution)/shard_map/all_to_all | solution.py:66
  476.1 1.2 copy.23
  477.3 2.9 while.38
  480.3 1.3 convolution_bitcast_fusion.1
  482.3 9.0 %all_to_all.35 = bf16[2,64,1024]{2,1,0:T(8,128)(2,1)S(1)} all-to-all(bf16[2,64,1024]{2,1,0:T(8,128)(2,1)S(1)} %copy_bitcast_fusion), channel_id=1, replica_groups=mesh['seq'=128,'head'=2] {'head'}, dimensions={0} | all-to-all | bytes 524288 | tf_op jit(solution)/shard_map/all_to_all | solution.py:93
  (373 shorter events, 172.8 us)
Async XLA Ops:
  2.0 0.7 copy-start
  47.9 411.2 %copy-start.3 = (bf16[128,1024]{1,0:T(8,128)(2,1)S(1)}, bf16[128,1024]{1,0:T(8,128)(2,1)}, u32[]{:S(2)}) copy-start(bf16[128,1024]{1,0:T(8,128)(2,1)} %param.12) | copy-start | bytes 786436
  47.9 190.9 %all-to-all-start = ((f32[128,128,128]{2,1,0:T(8,128)}), f32[128,128,128]{2,1,0:T(8,128)}, u32[]{:S(2)}, u32[]{:S(2)}) async-start(f32[128,128,128]{2,1,0:T(8,128)} %bitcast.86), calls=%async_computation | async-start | bytes 16777216 | tf_op jit(solution)/shard_map/all_to_all | solution.py:51
  451.5 23.8 %all-to-all-start.2 = ((f32[128,8,128]{2,1,0:T(8,128)}), f32[128,8,128]{2,1,0:T(8,128)S(1)}, u32[]{:S(2)}, u32[]{:S(2)}) async-start(f32[128,8,128]{2,1,0:T(8,128)} %get-tuple-element.89), calls=%async_computation.2 | async-start | bytes 1048576 | tf_op jit(solution)/shard_map/all_to_all | solution.py:66
  475.3 0.8 copy-start.2
  477.3 4.3 copy-start.1
  477.3 4.8 copy-start.4
where the time goes:
time: 498 us; the launch traced here: 492 us
  waiting for transfers between devices  199 us (40%)
  matrix products  136 us (27%)
  other arithmetic  83.6 us (17%)
  blocking collectives  44.5 us (9%)
  starting transfers between devices  15.2 us (3%)
  local copies, waits for them, and re-layouts  13.1 us (3%)
    all_to_all x1, waiting for transfers between devices, shards(): lax.all_to_all(outgoing_map, 'seq', split_axis=0, concat_axis=0, tiled=True)  183 us
    dot_general x128, matrix products, relay(): lax.dot_general(owner_state, source_map, (((1,), (1,)), ((), ())), precis...  130 us
    dynamic_update_slice x128, other arithmetic, shards(): lax.scan(relay, jnp.zeros((col_width, key_width), jnp.float32), (got_map,...  82.2 us
    all_to_all x1, blocking collectives, shards(): lax.all_to_all(send_upd, 'seq', split_axis=0, concat_axis=0, tiled=True)  35.4 us
    all_to_all x1, waiting for transfers between devices, shards(): lax.all_to_all(prefix, 'seq', split_axis=0, concat_axis=0, tiled=True)  16.1 us
  transfers between devices with their start and end apart: 2, of which 2 were waited for; matrix products, arithmetic and copies ran while one was open for 0% of the time, Pallas kernels for 0%

commit v1 on v0

v1 whole, which is shorter than its diff:
```python
import jax
import jax.numpy as jnp
from jax import lax
from jax.experimental import pallas as pl
from jax.experimental.pallas import tpu as pltpu
from jax.sharding import PartitionSpec as P

EPS = 1e-06
D = 128
ROWS = 2 * D + 16
F32 = jnp.float32
BF16 = jnp.bfloat16
VMEM = pl.BlockSpec(memory_space=pltpu.VMEM)
SMEM = pl.BlockSpec(memory_space=pltpu.SMEM)


def dot(a, b, ca, cb):
    return lax.dot_general(a, b, (((ca,), (cb,)), ((), ())), preferred_element_type=F32)


def eye_mask():
    return lax.broadcasted_iota(jnp.int32, (D, D), 0) == lax.broadcasted_iota(
        jnp.int32, (D, D), 1
    )


def split(matrix, eye):
    matrix = matrix.astype(F32)
    row = jnp.sum(jnp.where(eye, matrix, 0.0), axis=0, keepdims=True)
    return row, jnp.where(eye, 0.0, matrix).astype(BF16)


def pack(ref, at, matrix, state, eye):
    row, rest = split(matrix, eye)
    high = row.astype(BF16)
    low = (row - high.astype(F32)).astype(BF16)
    ref[(*at, pl.ds(0, D))] = rest
    ref[(*at, pl.ds(D, D))] = state.astype(BF16)
    tail = lax.broadcasted_iota(jnp.int32, (16, D), 0)
    both = jnp.where(tail == 0, high.astype(F32), jnp.where(tail == 1, low.astype(F32), 0.0))
    ref[(*at, pl.ds(2 * D, 16))] = both.astype(BF16)


def unpack(ref, at):
    rest = ref[(*at, pl.ds(0, D))]
    state = ref[(*at, pl.ds(D, D))].astype(F32)
    tail = ref[(*at, pl.ds(2 * D, 16))].astype(F32)
    row = tail[0:1] + tail[1:2]
    return row, rest, state


def local_compose(trans_ref, gate_ref, key_ref, value_ref, wire_ref):
    eye = eye_mask()
    heads = trans_ref.shape[1]
    rows = key_ref.shape[0] // 2
    for h in range(heads):
        cols = pl.ds(h * D, D)
        g0 = gate_ref[0, h]
        g1 = gate_ref[1, h]
        row0, rest0 = split(trans_ref[0, h], eye)
        row1, rest1 = split(trans_ref[1, h], eye)
        a1 = trans_ref[1, h]
        upd0 = dot(value_ref[pl.ds(0, rows), cols], key_ref[pl.ds(0, rows), cols], 0, 0)
        upd1 = dot(value_ref[pl.ds(rows, rows), cols], key_ref[pl.ds(rows, rows), cols], 0, 0)
        matrix = (g0 * g1) * (a1.astype(F32) * row0 + dot(a1, rest0, 1, 0))
        state = g1 * (upd0 * row1 + dot(upd0.astype(BF16), rest1, 1, 1)) + upd1
        pack(wire_ref, (h,), matrix, state, eye)


def group_prefix(wire_ref, pre_ref, total_ref):
    eye = eye_mask()
    count = wire_ref.shape[0]
    run = jnp.concatenate([eye.astype(F32), jnp.zeros((D, D), F32)], axis=0)
    for z in range(count):
        row, rest, state = unpack(wire_ref, (z,))
        pack(pre_ref, (z,), run[:D], run[D:], eye)
        run = run * row + dot(run.astype(BF16), rest, 1, 1)
        run = run + jnp.concatenate([jnp.zeros((D, D), F32), state], axis=0)
    pack(total_ref, (), run[:D], run[D:], eye)


def ring_prefix(axis, stride, own_ref, a_ref, b_ref, c_ref, pre_ref, total_ref, sorted_ref):
    eye = eye_mask()
    me = lax.rem(lax.axis_index(axis) // stride, 4)
    for d, ref in enumerate((own_ref, a_ref, b_ref, c_ref)):
        sorted_ref[lax.rem(me + 4 - d, 4)] = ref[...]
    run = jnp.concatenate([eye.astype(F32), jnp.zeros((D, D), F32)], axis=0)
    before = run
    for p in range(4):
        if p:
            before = jnp.where(me == p, run, before)
        row, rest, state = unpack(sorted_ref, (p,))
        run = run * row + dot(run.astype(BF16), rest, 1, 0)
        run = run + jnp.concatenate([jnp.zeros((D, D), F32), state], axis=0)
    pack(pre_ref, (), before[:D], before[D:], eye)
    pack(total_ref, (), run[:D], run[D:], eye)


def enter_states(
    axis, stride, own_ref, a_ref, b_ref, c_ref, outer_ref, pre_ref, state_ref, sorted_ref
):
    me = lax.rem(lax.axis_index(axis) // stride, 4)
    for d, ref in enumerate((own_ref, a_ref, b_ref, c_ref)):
        sorted_ref[lax.rem(me + 4 - d, 4)] = ref[...]

    def apply(run, ref, at):
        row, rest, state = unpack(ref, at)
        return run * row + dot(run.astype(BF16), rest, 1, 0) + state

    run = jnp.zeros((D, D), F32)
    before = run
    for p in range(3):
        run = apply(run, sorted_ref, (p,))
        before = jnp.where(me == p + 1, run, before)
    run = apply(before, outer_ref, ())
    for z in range(pre_ref.shape[0]):
        state_ref[z] = apply(run, pre_ref, (z,)).astype(BF16)


def outputs(
    query_ref, key_ref, value_ref, trans_ref, gate_ref, state_ref, gain_ref, out_ref
):
    eye = eye_mask()
    heads = trans_ref.shape[1]
    rows = key_ref.shape[0] // 2
    me = lax.axis_index("head")
    causal = lax.broadcasted_iota(jnp.int32, (rows, rows), 0) >= lax.broadcasted_iota(
        jnp.int32, (rows, rows), 1
    )
    gain = gain_ref[...]
    for h in range(heads):
        cols = pl.ds(h * D, D)
        entering = state_ref[h]
        row0, rest0 = split(trans_ref[0, h], eye)
        upd0 = dot(value_ref[pl.ds(0, rows), cols], key_ref[pl.ds(0, rows), cols], 0, 0)
        later = gate_ref[0, h] * (entering.astype(F32) * row0 + dot(entering, rest0, 1, 1)) + upd0
        for c, state in enumerate((entering, later.astype(BF16))):
            here = pl.ds(c * rows, rows)
            query = query_ref[here, cols]
            weights = jnp.where(causal, dot(query, key_ref[here, cols], 1, 1), 0.0).astype(BF16)
            mixed = dot(query, state, 1, 1) + dot(weights, value_ref[here, cols], 1, 0)
            factor = lax.rsqrt(jnp.mean(mixed * mixed, axis=-1, keepdims=True) + EPS)
            out_ref[lax.rem(me + c, 2), :, cols] = (mixed * factor * gain).astype(BF16)


def shards(queries, keys, values, transitions, gates, norm_gain):
    heads = transitions.shape[1]
    count = lax.axis_size("seq")
    lines = [[g * 8 + z for z in range(8)] for g in range(count // 8)]

    def around(stride, d):
        out = []
        for s in range(count):
            at = s // stride % 4
            out.append((s, s + ((at + d) % 4 - at) * stride))
        return out

    wire = pl.pallas_call(
        local_compose,
        out_shape=jax.ShapeDtypeStruct((heads, ROWS, D), BF16),
        in_specs=[VMEM, SMEM, VMEM, VMEM],
        out_specs=VMEM,
        name="local_compose",
    )(transitions, gates, keys, values)
    with jax.named_scope("to_owners"):
        wire = lax.all_to_all(wire, "seq", 0, 0, axis_index_groups=lines, tiled=True)
    one = jax.ShapeDtypeStruct((ROWS, D), BF16)
    pre, total = pl.pallas_call(
        group_prefix,
        out_shape=[jax.ShapeDtypeStruct(wire.shape, BF16), one],
        in_specs=[VMEM],
        out_specs=[VMEM, VMEM],
        name="group_prefix",
    )(wire)
    with jax.named_scope("along_y"):
        others = [lax.ppermute(total, "seq", around(8, d)) for d in (1, 2, 3)]
    outer, total = pl.pallas_call(
        lambda *refs: ring_prefix("seq", 8, *refs),
        out_shape=[one, one],
        in_specs=[VMEM] * 4,
        out_specs=[VMEM, VMEM],
        scratch_shapes=[pltpu.VMEM((4, ROWS, D), BF16)],
        name="ring_prefix",
    )(total, *others)
    with jax.named_scope("along_x"):
        others = [lax.ppermute(total, "seq", around(32, d)) for d in (1, 2, 3)]
    states = pl.pallas_call(
        lambda *refs: enter_states("seq", 32, *refs),
        out_shape=jax.ShapeDtypeStruct((wire.shape[0], D, D), BF16),
        in_specs=[VMEM] * 6,
        out_specs=VMEM,
        scratch_shapes=[pltpu.VMEM((4, ROWS, D), BF16)],
        name="enter_states",
    )(total, *others, outer, pre)
    with jax.named_scope("from_owners"):
        states = lax.all_to_all(states, "seq", 0, 0, axis_index_groups=lines, tiled=True)
    rows = queries.shape[0] // 2
    out = pl.pallas_call(
        outputs,
        out_shape=jax.ShapeDtypeStruct((2, rows, heads * D), BF16),
        in_specs=[VMEM, VMEM, VMEM, VMEM, SMEM, VMEM, VMEM],
        out_specs=VMEM,
        name="outputs",
    )(queries, keys, values, transitions, gates, states, norm_gain.reshape(1, D))
    with jax.named_scope("to_tokens"):
        other = lax.ppermute(out[1], "head", [(0, 1), (1, 0)])
    first = lax.axis_index("head") == 0
    return jnp.concatenate(
        [jnp.where(first, out[0], other), jnp.where(first, other, out[0])], axis=1
    )


def solution(mesh):
    placed = (
        P("seq", "head"),
        P("seq", "head"),
        P("seq", "head"),
        P("seq", "head", None, None),
        P("seq", "head"),
        P(),
    )
    return jax.shard_map(
        shards, mesh=mesh, in_specs=placed, out_specs=P(("seq", "head"), None), check_vma=False
    )
```

time: 498 us -> 79.4 us (0.16); the launches traced: 492 us -> 78.9 us
  waiting for transfers between devices: 199 us -> 5.75 us
  matrix products: 136 us -> 0 us
  other arithmetic: 83.6 us -> 0.74 us
  Pallas kernels: 0 us -> 14.3 us
  local copies, waits for them, and re-layouts: 13.1 us -> 2.24 us
  blocking collectives: 44.5 us -> 38.9 us
    all_to_all x2 -> x0, waiting for transfers between devices: 199 us -> none  [the longest x1 183 us: shards(): lax.all_to_all(outgoing_map, 'seq', split_axis=0, concat_axis=0, tiled=True)]
    dot_general x137 -> x0, matrix products: 136 us -> none  [the longest x128 130 us: relay(): lax.dot_general(owner_state, source_map, (((1,), (1,)), ((), ())), precis...]
    dynamic_update_slice x128 -> x0, other arithmetic: 82.2 us -> none  [shards(): lax.scan(relay, jnp.zeros((col_width, key_width), jnp.float32), (got_map,...]
    ppermute x0 -> x7, starting transfers between devices: none -> 16.9 us  [the longest x1 7.06 us: shards(): other = lax.ppermute(out[1], 'head', [(0, 1), (1, 0)])]
    all_to_all x2 -> x0, starting transfers between devices: 15.2 us -> none  [the longest x1 7.62 us: shards(): lax.all_to_all(outgoing_map, 'seq', split_axis=0, concat_axis=0, tiled=True)]
    pallas_call x0 -> x5, Pallas kernels: none -> 14.3 us  [the longest x1 3.89 us: shards(): pl.pallas_call(outputs, out_shape=jax.ShapeDtypeStruct((2, rows, heads *...]
    ppermute x0 -> x7, waiting for transfers between devices: none -> 5.75 us  [the longest x3 2.59 us: shards(): others = [lax.ppermute(total, 'seq', around(8, d)) for d in (1, 2, 3)]]
    all_to_all x2, blocking collectives: 44.5 us -> 38.9 us  [the longest x1 25.6 us: shards(): lax.all_to_all(wire, 'seq', 0, 0, axis_index_groups=lines, tiled=True)]
  transfers between devices with their start and end apart: 2 -> 7, of which waited for: 2 -> 5; matrix products, arithmetic and copies ran while one was open for 0% -> 0% of each run, Pallas kernels for 0% -> 0%
where the time goes in v1:
time: 79.4 us; the launch traced here: 78.9 us
  blocking collectives  38.9 us (49%)
  starting transfers between devices  16.9 us (21%)
  Pallas kernels  14.3 us (18%)
  waiting for transfers between devices  5.75 us (7%)
  local copies, waits for them, and re-layouts  2.24 us (3%)
    all_to_all x1, blocking collectives, shards(): lax.all_to_all(wire, 'seq', 0, 0, axis_index_groups=lines, tiled=True)  25.6 us
    all_to_all x1, blocking collectives, shards(): lax.all_to_all(states, 'seq', 0, 0, axis_index_groups=lines, tiled=True)  13.4 us
    ppermute x1, starting transfers between devices, shards(): other = lax.ppermute(out[1], 'head', [(0, 1), (1, 0)])  7.06 us
    ppermute x3, starting transfers between devices, shards(): others = [lax.ppermute(total, 'seq', around(8, d)) for d in (1, 2, 3)]  5.02 us
    ppermute x3, starting transfers between devices, shards(): others = [lax.ppermute(total, 'seq', around(32, d)) for d in (1, 2, 3)]  4.81 us
    pallas_call x1, Pallas kernels, shards(): pl.pallas_call(outputs, out_shape=jax.ShapeDtypeStruct((2, rows, heads *...  3.89 us
    pallas_call x1, Pallas kernels, shards(): pl.pallas_call(local_compose, out_shape=jax.ShapeDtypeStruct((heads, ROWS...  2.86 us
    pallas_call x1, Pallas kernels, shards(): pl.pallas_call(group_prefix, out_shape=[jax.ShapeDtypeStruct(wire.shape,...  2.77 us
  transfers between devices with their start and end apart: 7, of which 5 were waited for; matrix products, arithmetic and copies ran while one was open for 0% of the time, Pallas kernels for 0%

profile of v1, /device:TPU:1, one launch (start us, length us, event | category | flops | bytes accessed | tf_op | source)
XLA Modules:
  0.0 78.9 jit_solution(593747472261893797)
XLA Ops:
  0.0 2.9 %local_compose.1 = bf16[8,272,128]{2,1,0:T(8,128)(2,1)} custom-call(bf16[2,8,128,128]{3,2,1,0:T(8,128)(2,1)} %trans_ref.3, f32[2,8]{1,0:T(2,128)} %gate_ref.3, bf16[128,1024]{1,0:T(8,128)(2,1)} %key_ref.3, bf16[128,1024]{1,0:T(8,128)(2,1)} %value_ref.3), custom_call_target="tpu_custom_call" | custom-call | tf_op jit(solution)/shard_map/local_compose/pallas_call | solution.py:158
  2.9 25.6 %all_to_all.10.wire_ref = bf16[8,272,128]{2,1,0:T(8,128)(2,1)} all-to-all(bf16[8,272,128]{2,1,0:T(8,128)(2,1)} %local_compose.1), channel_id=1, replica_groups={{0,2,4,6,8,10,12,14},{16,18,20,22,24,26,28,30},{32,34,36,38,40,42,44,46..., dimensions={0} | all-to-all | bytes 1114112 | tf_op jit(solution)/shard_map/to_owners/all_to_all | solution.py:166
  28.4 2.8 %group_prefix.1 = (bf16[8,272,128]{2,1,0:T(8,128)(2,1)}, bf16[272,128]{1,0:T(8,128)(2,1)}) custom-call(bf16[8,272,128]{2,1,0:T(8,128)(2,1)} %all_to_all.10.wire_ref), custom_call_target="tpu_custom_call" | custom-call | tf_op jit(solution)/shard_map/group_prefix/pallas_call | solution.py:168
  31.2 1.3 %collective-permute-start = (bf16[272,128]{1,0:T(8,128)(2,1)}, bf16[272,128]{1,0:T(8,128)(2,1)S(1)}, u32[]{:S(2)}, u32[]{:S(2)}) collective-permute-start(bf16[272,128]{1,0:T(8,128)(2,1)} %get-tuple-element.9.refs_0_), channel_id=1, source_target_pairs={{0,16},{2,18},{4,20},{6,22},{8,24},{10,26},{12,28},{14,30},{16,32}... | collective-permute-start | bytes 208904 | tf_op jit(solution)/shard_map/along_y/ppermute | solution.py:176
  32.5 2.6 %collective-permute-start.1 = (bf16[272,128]{1,0:T(8,128)(2,1)}, bf16[272,128]{1,0:T(8,128)(2,1)S(1)}, u32[]{:S(2)}, u32[]{:S(2)}) collective-permute-start(bf16[272,128]{1,0:T(8,128)(2,1)} %get-tuple-element.9.refs_0_), channel_id=1, source_target_pairs={{0,32},{2,34},{4,36},{6,38},{8,40},{10,42},{12,44},{14,46},{16,48}... | collective-permute-start | bytes 208904 | tf_op jit(solution)/shard_map/along_y/ppermute | solution.py:176
  35.1 1.1 %collective-permute-start.2 = (bf16[272,128]{1,0:T(8,128)(2,1)}, bf16[272,128]{1,0:T(8,128)(2,1)S(1)}, u32[]{:S(2)}, u32[]{:S(2)}) collective-permute-start(bf16[272,128]{1,0:T(8,128)(2,1)} %get-tuple-element.9.refs_0_), channel_id=1, source_target_pairs={{0,48},{2,50},{4,52},{6,54},{8,56},{10,58},{12,60},{14,62},{16,0},... | collective-permute-start | bytes 208904 | tf_op jit(solution)/shard_map/along_y/ppermute | solution.py:176
  36.2 0.0 collective-permute-done.refs_1_
  36.2 0.0 copy-start.4
  36.2 1.6 %collective-permute-done.1.refs_2_ = bf16[272,128]{1,0:T(8,128)(2,1)S(1)} collective-permute-done((bf16[272,128]{1,0:T(8,128)(2,1)}, bf16[272,128]{1,0:T(8,128)(2,1)S(1)}, u32[]{:S(2)}, u32[]{:S(2)}) %collective-permute-start.1) | collective-permute-done | bytes 69664 | tf_op jit(solution)/shard_map/along_y/ppermute | solution.py:176
  37.8 0.0 copy-start.5
  37.8 1.0 %collective-permute-done.2.refs_3_ = bf16[272,128]{1,0:T(8,128)(2,1)S(1)} collective-permute-done((bf16[272,128]{1,0:T(8,128)(2,1)}, bf16[272,128]{1,0:T(8,128)(2,1)S(1)}, u32[]{:S(2)}, u32[]{:S(2)}) %collective-permute-start.2) | collective-permute-done | bytes 69664 | tf_op jit(solution)/shard_map/along_y/ppermute | solution.py:176
  38.8 0.0 copy-done.4
  38.8 0.0 copy-done.5
  38.8 0.0 copy-start.6
  38.8 0.6 copy-done.6
  39.4 2.2 %ring_prefix.1 = (bf16[272,128]{1,0:T(8,128)(2,1)}, bf16[272,128]{1,0:T(8,128)(2,1)}) custom-call(bf16[272,128]{1,0:T(8,128)(2,1)} %get-tuple-element.9.refs_0_, bf16[272,128]{1,0:T(8,128)(2,1)} %copy-done.4, bf16[272,128]{1,0:T(8,128)(2,1)} %copy-done.5, bf16[272,128]{1,0:T(8,128)(2,1)} %copy-done.6), custom_call_target="tpu_custom_call" | custom-call | tf_op jit(solution)/shard_map/ring_prefix/pallas_call | solution.py:177
  41.6 1.2 %collective-permute-start.3 = (bf16[272,128]{1,0:T(8,128)(2,1)}, bf16[272,128]{1,0:T(8,128)(2,1)S(1)}, u32[]{:S(2)}, u32[]{:S(2)}) collective-permute-start(bf16[272,128]{1,0:T(8,128)(2,1)} %get-tuple-element.10.refs_0_), channel_id=1, source_target_pairs={{0,64},{2,66},{4,68},{6,70},{8,72},{10,74},{12,76},{14,78},{16,80}... | collective-permute-start | bytes 208904 | tf_op jit(solution)/shard_map/along_x/ppermute | solution.py:186
  42.8 2.4 %collective-permute-start.4 = (bf16[272,128]{1,0:T(8,128)(2,1)}, bf16[272,128]{1,0:T(8,128)(2,1)S(1)}, u32[]{:S(2)}, u32[]{:S(2)}) collective-permute-start(bf16[272,128]{1,0:T(8,128)(2,1)} %get-tuple-element.10.refs_0_), channel_id=1, source_target_pairs={{0,128},{2,130},{4,132},{6,134},{8,136},{10,138},{12,140},{14,142}... | collective-permute-start | bytes 208904 | tf_op jit(solution)/shard_map/along_x/ppermute | solution.py:186
  45.2 1.2 %collective-permute-start.5 = (bf16[272,128]{1,0:T(8,128)(2,1)}, bf16[272,128]{1,0:T(8,128)(2,1)S(1)}, u32[]{:S(2)}, u32[]{:S(2)}) collective-permute-start(bf16[272,128]{1,0:T(8,128)(2,1)} %get-tuple-element.10.refs_0_), channel_id=1, source_target_pairs={{0,192},{2,194},{4,196},{6,198},{8,200},{10,202},{12,204},{14,206}... | collective-permute-start | bytes 208904 | tf_op jit(solution)/shard_map/along_x/ppermute | solution.py:186
  46.4 0.0 collective-permute-done.3.refs_1_
  46.4 0.0 copy-start.1
  46.4 1.5 %collective-permute-done.4.refs_2_ = bf16[272,128]{1,0:T(8,128)(2,1)S(1)} collective-permute-done((bf16[272,128]{1,0:T(8,128)(2,1)}, bf16[272,128]{1,0:T(8,128)(2,1)S(1)}, u32[]{:S(2)}, u32[]{:S(2)}) %collective-permute-start.4) | collective-permute-done | bytes 69664 | tf_op jit(solution)/shard_map/along_x/ppermute | solution.py:186
  47.9 0.0 copy-start.2
  47.9 0.7 collective-permute-done.5.refs_3_
  48.6 0.0 copy-start.3
  48.6 0.0 copy-done.1
  48.6 0.0 copy-done.2
  48.6 0.6 copy-done.3
  49.2 2.7 %enter_states.1 = bf16[8,128,128]{2,1,0:T(8,128)(2,1)} custom-call(bf16[272,128]{1,0:T(8,128)(2,1)} %get-tuple-element.10.refs_0_, bf16[272,128]{1,0:T(8,128)(2,1)} %copy-done.1, bf16[272,128]{1,0:T(8,128)(2,1)} %copy-done.2, bf16[272,128]{1,0:T(8,128)(2,1)} %copy-done.3, bf16[272,128]{1,0:T(8,128)(2,1)} %get-tuple-element.11.refs_4_, ...), custom_call_target="tpu_custom_call" | custom-call | tf_op jit(solution)/shard_map/enter_states/pallas_call | solution.py:187
  51.9 13.4 %all_to_all.11.state_ref = bf16[8,128,128]{2,1,0:T(8,128)(2,1)} all-to-all(bf16[8,128,128]{2,1,0:T(8,128)(2,1)} %enter_states.1), channel_id=1, replica_groups={{0,2,4,6,8,10,12,14},{16,18,20,22,24,26,28,30},{32,34,36,38,40,42,44,46..., dimensions={0} | all-to-all | bytes 524288 | tf_op jit(solution)/shard_map/from_owners/all_to_all | solution.py:196
  65.2 3.9 %outputs.1 = bf16[2,64,1024]{2,1,0:T(8,128)(2,1)} custom-call(bf16[128,1024]{1,0:T(8,128)(2,1)} %query_ref.1, bf16[128,1024]{1,0:T(8,128)(2,1)} %key_ref.3, bf16[128,1024]{1,0:T(8,128)(2,1)} %value_ref.3, bf16[2,8,128,128]{3,2,1,0:T(8,128)(2,1)} %trans_ref.3, f32[2,8]{1,0:T(2,128)} %gate_ref.3, bf16[8,128,128]{2,1,0:T(8,128)(2,1)} %all_to_all.11.state_ref, ...), custom_call_target="tpu_custom_call" | custom-call | tf_op jit(solution)/shard_map/outputs/pallas_call | solution.py:198
  69.1 0.0 copy-start
  69.1 1.0 %slice_bitcast_fusion = bf16[64,1024]{1,0:T(8,128)(2,1)S(1)} fusion(bf16[2,64,1024]{2,1,0:T(8,128)(2,1)} %outputs.1), kind=kLoop, calls=%fused_computation.1 | loop fusion | bytes 262144 | tf_op jit(solution)/shard_map/to_tokens/squeeze | solution.py:206
  70.1 7.1 %collective-permute-start.6 = (bf16[64,1024]{1,0:T(8,128)(2,1)S(1)}, bf16[64,1024]{1,0:T(8,128)(2,1)S(1)}, u32[]{:S(2)}, u32[]{:S(2)}) collective-permute-start(bf16[64,1024]{1,0:T(8,128)(2,1)S(1)} %slice_bitcast_fusion), channel_id=1, source_target_pairs={{0,1},{1,0},{2,3},{3,2},{4,5},{5,4},{6,7},{7,6},{8,9},{9,8},{10,11... | collective-permute-start | bytes 393224 | tf_op jit(solution)/shard_map/to_tokens/ppermute | solution.py:206
  77.2 1.0 %collective-permute-done.6 = bf16[64,1024]{1,0:T(8,128)(2,1)S(1)} collective-permute-done((bf16[64,1024]{1,0:T(8,128)(2,1)S(1)}, bf16[64,1024]{1,0:T(8,128)(2,1)S(1)}, u32[]{:S(2)}, u32[]{:S(2)}) %collective-permute-start.6) | collective-permute-done | bytes 131104 | tf_op jit(solution)/shard_map/to_tokens/ppermute | solution.py:206
  78.2 0.0 copy-done
  78.2 0.7 pad_maximum_fusion
  (1 shorter events, 0.0 us)
Async XLA Ops:
  31.2 5.0 %collective-permute-start = (bf16[272,128]{1,0:T(8,128)(2,1)}, bf16[272,128]{1,0:T(8,128)(2,1)S(1)}, u32[]{:S(2)}, u32[]{:S(2)}) collective-permute-start(bf16[272,128]{1,0:T(8,128)(2,1)} %get-tuple-element.9.refs_0_), channel_id=1, source_target_pairs={{0,16},{2,18},{4,20},{6,22},{8,24},{10,26},{12,28},{14,30},{16,32}... | collective-permute-start | bytes 208904 | tf_op jit(solution)/shard_map/along_y/ppermute | solution.py:176
  32.5 5.3 %collective-permute-start.1 = (bf16[272,128]{1,0:T(8,128)(2,1)}, bf16[272,128]{1,0:T(8,128)(2,1)S(1)}, u32[]{:S(2)}, u32[]{:S(2)}) collective-permute-start(bf16[272,128]{1,0:T(8,128)(2,1)} %get-tuple-element.9.refs_0_), channel_id=1, source_target_pairs={{0,32},{2,34},{4,36},{6,38},{8,40},{10,42},{12,44},{14,46},{16,48}... | collective-permute-start | bytes 208904 | tf_op jit(solution)/shard_map/along_y/ppermute | solution.py:176
  35.1 3.7 %collective-permute-start.2 = (bf16[272,128]{1,0:T(8,128)(2,1)}, bf16[272,128]{1,0:T(8,128)(2,1)S(1)}, u32[]{:S(2)}, u32[]{:S(2)}) collective-permute-start(bf16[272,128]{1,0:T(8,128)(2,1)} %get-tuple-element.9.refs_0_), channel_id=1, source_target_pairs={{0,48},{2,50},{4,52},{6,54},{8,56},{10,58},{12,60},{14,62},{16,0},... | collective-permute-start | bytes 208904 | tf_op jit(solution)/shard_map/along_y/ppermute | solution.py:176
  36.2 2.6 %copy-start.4 = (bf16[272,128]{1,0:T(8,128)(2,1)}, bf16[272,128]{1,0:T(8,128)(2,1)S(1)}, u32[]{:S(2)}) copy-start(bf16[272,128]{1,0:T(8,128)(2,1)S(1)} %collective-permute-done.refs_1_) | copy-start | bytes 208900
  37.8 1.0 %copy-start.5 = (bf16[272,128]{1,0:T(8,128)(2,1)}, bf16[272,128]{1,0:T(8,128)(2,1)S(1)}, u32[]{:S(2)}) copy-start(bf16[272,128]{1,0:T(8,128)(2,1)S(1)} %collective-permute-done.1.refs_2_) | copy-start | bytes 208900
  38.8 0.6 copy-start.6
  41.6 4.8 %collective-permute-start.3 = (bf16[272,128]{1,0:T(8,128)(2,1)}, bf16[272,128]{1,0:T(8,128)(2,1)S(1)}, u32[]{:S(2)}, u32[]{:S(2)}) collective-permute-start(bf16[272,128]{1,0:T(8,128)(2,1)} %get-tuple-element.10.refs_0_), channel_id=1, source_target_pairs={{0,64},{2,66},{4,68},{6,70},{8,72},{10,74},{12,76},{14,78},{16,80}... | collective-permute-start | bytes 208904 | tf_op jit(solution)/shard_map/along_x/ppermute | solution.py:186
  42.8 5.1 %collective-permute-start.4 = (bf16[272,128]{1,0:T(8,128)(2,1)}, bf16[272,128]{1,0:T(8,128)(2,1)S(1)}, u32[]{:S(2)}, u32[]{:S(2)}) collective-permute-start(bf16[272,128]{1,0:T(8,128)(2,1)} %get-tuple-element.10.refs_0_), channel_id=1, source_target_pairs={{0,128},{2,130},{4,132},{6,134},{8,136},{10,138},{12,140},{14,142}... | collective-permute-start | bytes 208904 | tf_op jit(solution)/shard_map/along_x/ppermute | solution.py:186
  45.2 3.4 %collective-permute-start.5 = (bf16[272,128]{1,0:T(8,128)(2,1)}, bf16[272,128]{1,0:T(8,128)(2,1)S(1)}, u32[]{:S(2)}, u32[]{:S(2)}) collective-permute-start(bf16[272,128]{1,0:T(8,128)(2,1)} %get-tuple-element.10.refs_0_), channel_id=1, source_target_pairs={{0,192},{2,194},{4,196},{6,198},{8,200},{10,202},{12,204},{14,206}... | collective-permute-start | bytes 208904 | tf_op jit(solution)/shard_map/along_x/ppermute | solution.py:186
  46.4 2.2 %copy-start.1 = (bf16[272,128]{1,0:T(8,128)(2,1)}, bf16[272,128]{1,0:T(8,128)(2,1)S(1)}, u32[]{:S(2)}) copy-start(bf16[272,128]{1,0:T(8,128)(2,1)S(1)} %collective-permute-done.3.refs_1_) | copy-start | bytes 208900
  47.9 0.7 copy-start.2
  48.6 0.6 copy-start.3
  69.1 9.0 %copy-start = (bf16[2,64,1024]{2,1,0:T(8,128)(2,1)S(1)}, bf16[2,64,1024]{2,1,0:T(8,128)(2,1)}, u32[]{:S(2)}) copy-start(bf16[2,64,1024]{2,1,0:T(8,128)(2,1)} %outputs.1) | copy-start | bytes 786436
  70.1 8.0 %collective-permute-start.6 = (bf16[64,1024]{1,0:T(8,128)(2,1)S(1)}, bf16[64,1024]{1,0:T(8,128)(2,1)S(1)}, u32[]{:S(2)}, u32[]{:S(2)}) collective-permute-start(bf16[64,1024]{1,0:T(8,128)(2,1)S(1)} %slice_bitcast_fusion), channel_id=1, source_target_pairs={{0,1},{1,0},{2,3},{3,2},{4,5},{5,4},{6,7},{7,6},{8,9},{9,8},{10,11... | collective-permute-start | bytes 393224 | tf_op jit(solution)/shard_map/to_tokens/ppermute | solution.py:206

commit v2 on v0

v2 whole, which is shorter than its diff:
```python
import jax
import jax.numpy as jnp
from jax import lax
from jax.experimental import pallas as pl
from jax.experimental.pallas import tpu as pltpu
from jax.sharding import PartitionSpec as P

EPS = 1e-06
D = 128
ROWS = 2 * D + 16
F32 = jnp.float32
BF16 = jnp.bfloat16
VMEM = pl.BlockSpec(memory_space=pltpu.VMEM)
PLAIN = pl.BlockSpec(memory_space=pltpu.VMEM)
SMEM = pl.BlockSpec(memory_space=pltpu.SMEM)
ANY = pl.BlockSpec(memory_space=pl.ANY)


def dot(a, b, ca, cb):
    return lax.dot_general(a, b, (((ca,), (cb,)), ((), ())), preferred_element_type=F32)


def eye_mask():
    return lax.broadcasted_iota(jnp.int32, (D, D), 0) == lax.broadcasted_iota(
        jnp.int32, (D, D), 1
    )


def split(matrix, eye):
    matrix = matrix.astype(F32)
    row = jnp.sum(jnp.where(eye, matrix, 0.0), axis=0, keepdims=True)
    return row, jnp.where(eye, 0.0, matrix).astype(BF16)


def pack(ref, at, both, eye):
    row, rest = split(both[:D], eye)
    high = row.astype(BF16)
    low = (row - high.astype(F32)).astype(BF16)
    ref[(*at, pl.ds(0, D))] = rest
    ref[(*at, pl.ds(D, D))] = both[D:].astype(BF16)
    place = lax.broadcasted_iota(jnp.int32, (16, D), 0)
    tail = jnp.where(place == 0, high.astype(F32), jnp.where(place == 1, low.astype(F32), 0.0))
    ref[(*at, pl.ds(2 * D, 16))] = tail.astype(BF16)


def unpack(ref, at=()):
    tail = ref[(*at, pl.ds(2 * D, 16))].astype(F32)
    rest = ref[(*at, pl.ds(0, D))]
    return tail[0:1] + tail[1:2], rest, ref[(*at, pl.ds(D, D))].astype(F32)


def dense(parts, eye):
    row, rest, state = parts
    return jnp.concatenate([jnp.where(eye, row, rest.astype(F32)), state], axis=0)


def divide(both, eye):
    return (*split(both[:D], eye), both[D:])


def then(both, parts):
    row, rest, state = parts
    after = both * row + dot(both.astype(BF16), rest, 1, 0)
    return jnp.concatenate([after[:D], after[D:] + state], axis=0)


def advance(state, parts):
    row, rest, add = parts
    return state * row + dot(state.astype(BF16), rest, 1, 0) + add


def local_compose(
    trans_hbm, gate_ref, key_hbm, value_hbm, wire_ref, trans_ref, key_ref, value_ref, sems
):
    heads = range(trans_ref.shape[1])
    rows = key_ref.shape[0] // 2
    pairs = (
        (key_hbm, key_ref),
        (value_hbm, value_ref),
        (trans_hbm.at[1], trans_ref.at[1]),
        (trans_hbm.at[0], trans_ref.at[0]),
    )
    copies = [pltpu.make_async_copy(*pair, sems.at[i]) for i, pair in enumerate(pairs)]
    for copy in copies:
        copy.start()
    eye = eye_mask()
    copies[0].wait()
    copies[1].wait()

    def update(c, h):
        here = (pl.ds(c * rows, rows), pl.ds(h * D, D))
        return dot(value_ref[here], key_ref[here], 0, 0)

    updates = [(update(0, h), update(1, h)) for h in heads]
    copies[2].wait()
    states = []
    for h in heads:
        upd0, upd1 = updates[h]
        high = upd0.astype(BF16)
        low = (upd0 - high.astype(F32)).astype(BF16)
        moved = dot(jnp.concatenate([high, low], axis=0), trans_ref[1, h], 1, 1)
        states.append(gate_ref[1, h] * (moved[:D] + moved[D:]) + upd1)
    copies[3].wait()
    for h in heads:
        matrix = dot(trans_ref[0, h], trans_ref[1, h], 0, 1)
        matrix = (gate_ref[0, h] * gate_ref[1, h]) * matrix
        pack(wire_ref, (h,), jnp.concatenate([matrix, states[h]], axis=0), eye)


def line_total(wire_ref, total_ref):
    eye = eye_mask()
    count = wire_ref.shape[0]
    runs = [
        then(dense(unpack(wire_ref, (z,)), eye), unpack(wire_ref, (z + 1,)))
        for z in range(0, count, 2)
    ]
    while len(runs) > 1:
        runs = [then(runs[i], divide(runs[i + 1], eye)) for i in range(0, len(runs), 2)]
    pack(total_ref, (), runs[0], eye)


def line_before(wire_ref, gain_in_ref, pre_ref, gain_ref):
    gain_ref[...] = gain_in_ref[...]
    eye = eye_mask()
    run = jnp.concatenate([eye.astype(F32), jnp.zeros((D, D), F32)], axis=0)
    for z in range(wire_ref.shape[0]):
        pack(pre_ref, (z,), run, eye)
        if z == 0:
            run = dense(unpack(wire_ref, (0,)), eye)
        elif z < wire_ref.shape[0] - 1:
            run = then(run, unpack(wire_ref, (z,)))


def sort_ring(stride, refs, sorted_ref):
    me = lax.rem(lax.axis_index("seq") // stride, 4)
    for d, ref in zip((0, 3, 1, 2), refs):
        sorted_ref[lax.rem(me + 4 - d, 4)] = ref[...]
    return me


def plane_total(own_ref, a_ref, b_ref, c_ref, total_ref, sorted_ref):
    eye = eye_mask()
    sort_ring(8, (own_ref, a_ref, b_ref, c_ref), sorted_ref)
    one = then(dense(unpack(sorted_ref, (0,)), eye), unpack(sorted_ref, (1,)))
    two = then(dense(unpack(sorted_ref, (2,)), eye), unpack(sorted_ref, (3,)))
    pack(total_ref, (), then(one, divide(two, eye)), eye)


def plane_before(own_ref, a_ref, b_ref, c_ref, pre_ref, sorted_ref):
    eye = eye_mask()
    me = sort_ring(8, (own_ref, a_ref, b_ref, c_ref), sorted_ref)
    before = jnp.concatenate([eye.astype(F32), jnp.zeros((D, D), F32)], axis=0)
    run = dense(unpack(sorted_ref, (0,)), eye)
    before = jnp.where(me == 1, run, before)
    for y in (1, 2):
        run = then(run, unpack(sorted_ref, (y,)))
        before = jnp.where(me == y + 1, run, before)
    pack(pre_ref, (), before, eye)


def enter_states(own_ref, a_ref, b_ref, c_ref, plane_ref, line_ref, state_ref, sorted_ref):
    me = sort_ring(32, (own_ref, a_ref, b_ref, c_ref), sorted_ref)
    run = sorted_ref[0, pl.ds(D, D)].astype(F32)
    before = jnp.where(me == 1, run, 0.0)
    for x in (1, 2):
        run = advance(run, unpack(sorted_ref, (x,)))
        before = jnp.where(me == x + 1, run, before)
    run = advance(before, unpack(plane_ref))
    for z in range(line_ref.shape[0]):
        state_ref[z] = advance(run, unpack(line_ref, (z,))).astype(BF16)


def normed_block(block, query_ref, key_ref, value_ref, state_ref, gain_ref, out_ref):
    rows = key_ref.shape[0] // 2
    here = pl.ds(pl.multiple_of(block * rows, rows), rows)
    causal = lax.broadcasted_iota(jnp.int32, (rows, rows), 0) >= lax.broadcasted_iota(
        jnp.int32, (rows, rows), 1
    )
    gain = gain_ref[...]
    heads = range(state_ref.shape[0])
    cols = [pl.ds(h * D, D) for h in heads]
    scores = [dot(query_ref[here, c], key_ref[here, c], 1, 1) for c in cols]
    weights = [jnp.where(causal, x, 0.0).astype(BF16) for x in scores]
    mixed = [
        dot(query_ref[here, c], state_ref[h], 1, 1) + dot(w, value_ref[here, c], 1, 0)
        for h, c, w in zip(heads, cols, weights)
    ]
    for h in heads:
        mean = jnp.mean(mixed[h] * mixed[h], axis=-1, keepdims=True)
        out_ref(h, (mixed[h] * lax.rsqrt(mean + EPS) * gain).astype(BF16))


def sent_outputs(
    query_ref, key_ref, value_ref, trans_ref, gate_ref, state_ref, gain_ref,
    send_ref, kept_ref, used_ref,
):
    rows = key_ref.shape[0] // 2
    me = lax.axis_index("head")
    for h in range(state_ref.shape[0]):
        cols = pl.ds(h * D, D)
        entering = state_ref[h]
        upd = dot(value_ref[pl.ds(0, rows), cols], key_ref[pl.ds(0, rows), cols], 0, 0)
        later = gate_ref[0, h] * dot(entering, trans_ref[0, h], 1, 1) + upd
        first = entering.astype(F32)
        used_ref[h] = jnp.where(me == 0, later, first).astype(BF16)
        kept_ref[h] = jnp.where(me == 0, first, later).astype(BF16)

    def write(h, value):
        send_ref[:, pl.ds(h * D, D)] = value

    normed_block(1 - me, query_ref, key_ref, value_ref, used_ref, gain_ref, write)


def kept_outputs(query_ref, key_ref, value_ref, state_ref, gain_ref, out_ref):
    me = lax.axis_index("head")
    start = me * (state_ref.shape[0] * D)

    def write(h, value):
        out_ref[:, pl.ds(pl.multiple_of(start + h * D, D), D)] = value

    normed_block(me, query_ref, key_ref, value_ref, state_ref, gain_ref, write)


def call(kernel, outs, *operands, scratch=(), flops=0, specs=None):
    shapes = [
        jax.ShapeDtypeStruct(*out[:2]) if len(out) > 2 else pltpu.VMEM(*out) for out in outs
    ]
    specs = specs or [VMEM] * len(operands)
    operands = [
        pltpu.with_memory_space_constraint(x, pltpu.VMEM) if spec is VMEM else x
        for x, spec in zip(operands, specs)
    ]
    return pl.pallas_call(
        kernel,
        out_shape=shapes,
        in_specs=specs,
        out_specs=[VMEM] * len(outs),
        scratch_shapes=scratch,
        cost_estimate=pl.CostEstimate(flops=flops, bytes_accessed=1 << 20, transcendentals=0),
        name=kernel.__name__,
    )(*operands)


def shards(queries, keys, values, transitions, gates, norm_gain):
    heads = transitions.shape[1]
    count = lax.axis_size("seq")
    tokens = queries.shape[0]
    lines = [[g * 8 + z for z in range(8)] for g in range(count // 8)]
    line = ((heads, ROWS, D), BF16)
    one = ((ROWS, D), BF16)
    ring = [pltpu.VMEM((4, ROWS, D), BF16)]

    def around(total, stride):
        out = []
        for d in (3, 1, 2):
            pairs = []
            for s in range(count):
                at = s // stride % 4
                pairs.append((s, s + ((at + d) % 4 - at) * stride))
            out.append(lax.ppermute(total, "seq", pairs))
        return lax.optimization_barrier(out)

    (wire,) = call(
        local_compose, [line], transitions, gates, keys, values, specs=[ANY, SMEM, ANY, ANY],
        scratch=[
            pltpu.VMEM(transitions.shape, BF16),
            pltpu.VMEM(keys.shape, BF16),
            pltpu.VMEM(values.shape, BF16),
            pltpu.SemaphoreType.DMA((4,)),
        ],
    )
    with jax.named_scope("to_owners"):
        wire = lax.all_to_all(wire, "seq", 0, 0, axis_index_groups=lines, tiled=True)
    (total,) = call(line_total, [one], wire)
    with jax.named_scope("along_y"):
        others = around(total, 8)
    line_pre, gain = call(
        line_before, [line, ((1, D), F32)], wire, norm_gain.reshape(1, D), specs=[VMEM, PLAIN]
    )
    (whole,) = call(plane_total, [one], total, *others, scratch=ring)
    with jax.named_scope("along_x"):
        planes = around(whole, 32)
    (plane_pre,) = call(plane_before, [one], total, *others, scratch=ring)
    (states,) = call(
        enter_states, [((heads, D, D), BF16)], whole, *planes, plane_pre, line_pre, scratch=ring
    )
    with jax.named_scope("from_owners"):
        states = lax.all_to_all(states, "seq", 0, 0, axis_index_groups=lines, tiled=True)
    half = (tokens // 2, heads * D)
    send, kept = call(
        sent_outputs,
        [(half, BF16), ((heads, D, D), BF16)],
        queries, keys, values, transitions, gates, states, gain,
        specs=[VMEM] * 4 + [SMEM] + [VMEM] * 2,
        scratch=[pltpu.VMEM((heads, D, D), BF16)],
    )
    with jax.named_scope("to_tokens"):
        other = lax.ppermute(send, "head", [(0, 1), (1, 0)])
    (out,) = call(
        kept_outputs, [((tokens // 2, 2 * heads * D), BF16, "hbm")],
        queries, keys, values, kept, gain,
    )
    there = (1 - lax.axis_index("head")) * (heads * D)
    return lax.dynamic_update_slice(out, other, (0, there))


def solution(mesh):
    placed = (
        P("seq", "head"),
        P("seq", "head"),
        P("seq", "head"),
        P("seq", "head", None, None),
        P("seq", "head"),
        P(),
    )
    return jax.shard_map(
        shards, mesh=mesh, in_specs=placed, out_specs=P(("seq", "head"), None), check_vma=False
    )
```

time: 498 us -> 66.5 us (0.13); the launches traced: 492 us -> 66.3 us
  waiting for transfers between devices: 199 us -> 2.51 us
  matrix products: 136 us -> 0 us
  other arithmetic: 83.6 us -> 0 us
  local copies, waits for them, and re-layouts: 13.1 us -> 0.69 us
  Pallas kernels: 0 us -> 8.77 us
  blocking collectives: 44.5 us -> 37.6 us
    all_to_all x2 -> x0, waiting for transfers between devices: 199 us -> none  [the longest x1 183 us: shards(): lax.all_to_all(outgoing_map, 'seq', split_axis=0, concat_axis=0, tiled=True)]
    dot_general x137 -> x0, matrix products: 136 us -> none  [the longest x128 130 us: relay(): lax.dot_general(owner_state, source_map, (((1,), (1,)), ((), ())), precis...]
    dynamic_update_slice x128 -> x0, other arithmetic: 82.2 us -> none  [shards(): lax.scan(relay, jnp.zeros((col_width, key_width), jnp.float32), (got_map,...]
    ppermute x0 -> x7, starting transfers between devices: none -> 16.6 us  [the longest x6 11.2 us: around(): out.append(lax.ppermute(total, 'seq', pairs))]
    all_to_all x2 -> x0, starting transfers between devices: 15.2 us -> none  [the longest x1 7.62 us: shards(): lax.all_to_all(outgoing_map, 'seq', split_axis=0, concat_axis=0, tiled=True)]
    pallas_call x0 -> x8, Pallas kernels: none -> 8.77 us  [call(): pl.pallas_call(kernel, out_shape=shapes, in_specs=specs, out_specs=[VMEM]...]
    all_to_all x2, blocking collectives: 44.5 us -> 37.6 us  [the longest x1 25.3 us: shards(): lax.all_to_all(wire, 'seq', 0, 0, axis_index_groups=lines, tiled=True)]
  transfers between devices with their start and end apart: 2 -> 7, of which waited for: 2 -> 1; matrix products, arithmetic and copies ran while one was open for 0% -> 0% of each run, Pallas kernels for 0% -> 5%
where the time goes in v2:
time: 66.5 us; the launch traced here: 66.3 us
  blocking collectives  37.6 us (57%)
  starting transfers between devices  16.6 us (25%)
  Pallas kernels  8.77 us (13%)
  waiting for transfers between devices  2.51 us (4%)
  local copies, waits for them, and re-layouts  0.69 us (1%)
    all_to_all x1, blocking collectives, shards(): lax.all_to_all(wire, 'seq', 0, 0, axis_index_groups=lines, tiled=True)  25.3 us
    all_to_all x1, blocking collectives, shards(): lax.all_to_all(states, 'seq', 0, 0, axis_index_groups=lines, tiled=True)  12.3 us
    ppermute x6, starting transfers between devices, around(): out.append(lax.ppermute(total, 'seq', pairs))  11.2 us
    pallas_call x8, Pallas kernels, call(): pl.pallas_call(kernel, out_shape=shapes, in_specs=specs, out_specs=[VMEM]...  8.77 us
    ppermute x1, starting transfers between devices, shards(): other = lax.ppermute(send, 'head', [(0, 1), (1, 0)])  5.4 us
    ppermute x6, waiting for transfers between devices, around(): out.append(lax.ppermute(total, 'seq', pairs))  2.51 us
  transfers between devices with their start and end apart: 7, of which 1 were waited for; matrix products, arithmetic and copies ran while one was open for 0% of the time, Pallas kernels for 5%

profile of v2, /device:TPU:1, one launch (start us, length us, event | category | flops | bytes accessed | tf_op | source)
XLA Modules:
  0.0 66.3 jit_solution(7967953733582396359)
XLA Ops:
  0.0 2.8 %local_compose.1 = bf16[8,272,128]{2,1,0:T(8,128)(2,1)S(1)} custom-call(bf16[2,8,128,128]{3,2,1,0:T(8,128)(2,1)} %trans_ref.1, f32[2,8]{1,0:T(2,128)} %gate_ref.3, bf16[128,1024]{1,0:T(8,128)(2,1)} %key_ref.3, bf16[128,1024]{1,0:T(8,128)(2,1)} %value_ref.3), custom_call_target="tpu_custom_call" | custom-call | bytes 1048576 | tf_op jit(solution)/shard_map/local_compose/pallas_call | solution.py:233
  2.8 25.3 %all_to_all.10.wire_ref = bf16[8,272,128]{2,1,0:T(8,128)(2,1)S(1)} all-to-all(bf16[8,272,128]{2,1,0:T(8,128)(2,1)S(1)} %local_compose.1), channel_id=1, replica_groups={{0,2,4,6,8,10,12,14},{16,18,20,22,24,26,28,30},{32,34,36,38,40,42,44,46..., dimensions={0} | all-to-all | bytes 1114112 | tf_op jit(solution)/shard_map/to_owners/all_to_all | solution.py:273
  28.0 0.5 line_total.1.own_ref
  28.6 3.0 %collective-permute-start.2 = (bf16[272,128]{1,0:T(8,128)(2,1)S(1)}, bf16[272,128]{1,0:T(8,128)(2,1)S(1)}, u32[]{:S(2)}, u32[]{:S(2)}) collective-permute-start(bf16[272,128]{1,0:T(8,128)(2,1)S(1)} %line_total.1.own_ref), channel_id=1, source_target_pairs={{0,32},{2,34},{4,36},{6,38},{8,40},{10,42},{12,44},{14,46},{16,48}... | collective-permute-start | bytes 208904 | tf_op jit(solution)/shard_map/along_y/ppermute | solution.py:260
  31.6 0.4 collective-permute-start.1
  32.0 2.3 %collective-permute-start = (bf16[272,128]{1,0:T(8,128)(2,1)S(1)}, bf16[272,128]{1,0:T(8,128)(2,1)S(1)}, u32[]{:S(2)}, u32[]{:S(2)}) collective-permute-start(bf16[272,128]{1,0:T(8,128)(2,1)S(1)} %line_total.1.own_ref), channel_id=1, source_target_pairs={{0,48},{2,50},{4,52},{6,54},{8,56},{10,58},{12,60},{14,62},{16,0},... | collective-permute-start | bytes 208904 | tf_op jit(solution)/shard_map/along_y/ppermute | solution.py:260
  34.3 0.0 collective-permute-done.2.c_ref
  34.3 2.5 %collective-permute-done.1.b_ref = bf16[272,128]{1,0:T(8,128)(2,1)S(1)} collective-permute-done((bf16[272,128]{1,0:T(8,128)(2,1)S(1)}, bf16[272,128]{1,0:T(8,128)(2,1)S(1)}, u32[]{:S(2)}, u32[]{:S(2)}) %collective-permute-start.1) | collective-permute-done | bytes 69664 | tf_op jit(solution)/shard_map/along_y/ppermute | solution.py:260
  36.8 0.0 collective-permute-done.a_ref
  36.8 0.4 plane_total.1.own_ref
  37.2 2.8 %collective-permute-start.5 = (bf16[272,128]{1,0:T(8,128)(2,1)S(1)}, bf16[272,128]{1,0:T(8,128)(2,1)S(1)}, u32[]{:S(2)}, u32[]{:S(2)}) collective-permute-start(bf16[272,128]{1,0:T(8,128)(2,1)S(1)} %plane_total.1.own_ref), channel_id=1, source_target_pairs={{0,128},{2,130},{4,132},{6,134},{8,136},{10,138},{12,140},{14,142}... | collective-permute-start | bytes 208904 | tf_op jit(solution)/shard_map/along_x/ppermute | solution.py:260
  40.0 0.3 collective-permute-start.4
  40.3 2.4 %collective-permute-start.3 = (bf16[272,128]{1,0:T(8,128)(2,1)S(1)}, bf16[272,128]{1,0:T(8,128)(2,1)S(1)}, u32[]{:S(2)}, u32[]{:S(2)}) collective-permute-start(bf16[272,128]{1,0:T(8,128)(2,1)S(1)} %plane_total.1.own_ref), channel_id=1, source_target_pairs={{0,192},{2,194},{4,196},{6,198},{8,200},{10,202},{12,204},{14,206}... | collective-permute-start | bytes 208904 | tf_op jit(solution)/shard_map/along_x/ppermute | solution.py:260
  42.7 1.4 %line_before.1 = (bf16[8,272,128]{2,1,0:T(8,128)(2,1)S(1)}, f32[1,128]{1,0:T(1,128)S(1)}) custom-call(bf16[8,272,128]{2,1,0:T(8,128)(2,1)S(1)} %all_to_all.10.wire_ref, f32[1,128]{1,0:T(1,128)} %bitcast.1), custom_call_target="tpu_custom_call" | custom-call | bytes 1048576 | tf_op jit(solution)/shard_map/line_before/pallas_call | solution.py:233
  44.1 0.3 plane_before.1.plane_ref
  44.4 0.0 collective-permute-done.5.c_ref
  44.4 0.0 collective-permute-done.4.b_ref
  44.5 0.0 collective-permute-done.3.a_ref
  44.5 0.0 copy-start.2
  44.5 0.0 copy-start.3
  44.5 0.6 enter_states.1
  45.1 0.0 copy-start
  45.1 0.0 copy-start.1
  45.2 12.3 %all_to_all.11.state_ref = bf16[8,128,128]{2,1,0:T(8,128)(2,1)S(1)} all-to-all(bf16[8,128,128]{2,1,0:T(8,128)(2,1)S(1)} %enter_states.1), channel_id=1, replica_groups={{0,2,4,6,8,10,12,14},{16,18,20,22,24,26,28,30},{32,34,36,38,40,42,44,46..., dimensions={0} | all-to-all | bytes 524288 | tf_op jit(solution)/shard_map/from_owners/all_to_all | solution.py:288
  57.5 0.0 copy-done.2
  57.5 0.0 copy-done.3
  57.5 0.0 copy-done
  57.5 0.0 copy-done.1
  57.5 1.5 %sent_outputs.1 = (bf16[64,1024]{1,0:T(8,128)(2,1)S(1)}, bf16[8,128,128]{2,1,0:T(8,128)(2,1)S(1)}) custom-call(bf16[128,1024]{1,0:T(8,128)(2,1)S(1)} %copy-done.3, bf16[128,1024]{1,0:T(8,128)(2,1)S(1)} %copy-done, bf16[128,1024]{1,0:T(8,128)(2,1)S(1)} %copy-done.1, bf16[2,8,128,128]{3,2,1,0:T(8,128)(2,1)S(1)} %copy-done.2, f32[2,8]{1,0:T(2,128)} %gate_ref.3, ...), custom_call_target="tpu_custom_call" | custom-call | bytes 1048576 | tf_op jit(solution)/shard_map/sent_outputs/pallas_call | solution.py:233
  59.0 5.4 %collective-permute-start.6 = (bf16[64,1024]{1,0:T(8,128)(2,1)S(1)}, bf16[64,1024]{1,0:T(8,128)(2,1)S(1)}, u32[]{:S(2)}, u32[]{:S(2)}) collective-permute-start(bf16[64,1024]{1,0:T(8,128)(2,1)S(1)} %get-tuple-element.24), channel_id=1, source_target_pairs={{0,1},{1,0},{2,3},{3,2},{4,5},{5,4},{6,7},{7,6},{8,9},{9,8},{10,11... | collective-permute-start | bytes 393224 | tf_op jit(solution)/shard_map/to_tokens/ppermute | solution.py:298
  64.4 1.3 %kept_outputs.1 = bf16[64,2048]{1,0:T(8,128)(2,1)} custom-call(bf16[128,1024]{1,0:T(8,128)(2,1)S(1)} %copy-done.3, bf16[128,1024]{1,0:T(8,128)(2,1)S(1)} %copy-done, bf16[128,1024]{1,0:T(8,128)(2,1)S(1)} %copy-done.1, bf16[8,128,128]{2,1,0:T(8,128)(2,1)S(1)} %get-tuple-element.23.state_ref, f32[1,128]{1,0:T(1,128)S(1)} %get-tuple-element.22.gain_ref), custom_call_target="tpu_custom_call" | custom-call | bytes 1048576 | tf_op jit(solution)/shard_map/kept_outputs/pallas_call | solution.py:233
  65.6 0.0 collective-permute-done.6
  65.6 0.7 %constant_dynamic-update-slice_fusion = bf16[64,2048]{1,0:T(8,128)(2,1)} fusion(bf16[64,2048]{1,0:T(8,128)(2,1)} %kept_outputs.1, bf16[64,1024]{1,0:T(8,128)(2,1)S(1)} %collective-permute-done.6, s32[]{:T(128)S(6)} %select_n.3), kind=kLoop, calls=%fused_computation | loop fusion | bytes 262148 | tf_op jit(solution)/shard_map/dynamic_update_slice | solution.py:304
Async XLA Ops:
  28.6 5.7 %collective-permute-start.2 = (bf16[272,128]{1,0:T(8,128)(2,1)S(1)}, bf16[272,128]{1,0:T(8,128)(2,1)S(1)}, u32[]{:S(2)}, u32[]{:S(2)}) collective-permute-start(bf16[272,128]{1,0:T(8,128)(2,1)S(1)} %line_total.1.own_ref), channel_id=1, source_target_pairs={{0,32},{2,34},{4,36},{6,38},{8,40},{10,42},{12,44},{14,46},{16,48}... | collective-permute-start | bytes 208904 | tf_op jit(solution)/shard_map/along_y/ppermute | solution.py:260
  31.6 5.2 %collective-permute-start.1 = (bf16[272,128]{1,0:T(8,128)(2,1)S(1)}, bf16[272,128]{1,0:T(8,128)(2,1)S(1)}, u32[]{:S(2)}, u32[]{:S(2)}) collective-permute-start(bf16[272,128]{1,0:T(8,128)(2,1)S(1)} %line_total.1.own_ref), channel_id=1, source_target_pairs={{0,16},{2,18},{4,20},{6,22},{8,24},{10,26},{12,28},{14,30},{16,32}... | collective-permute-start | bytes 208904 | tf_op jit(solution)/shard_map/along_y/ppermute | solution.py:260
  32.0 4.8 %collective-permute-start = (bf16[272,128]{1,0:T(8,128)(2,1)S(1)}, bf16[272,128]{1,0:T(8,128)(2,1)S(1)}, u32[]{:S(2)}, u32[]{:S(2)}) collective-permute-start(bf16[272,128]{1,0:T(8,128)(2,1)S(1)} %line_total.1.own_ref), channel_id=1, source_target_pairs={{0,48},{2,50},{4,52},{6,54},{8,56},{10,58},{12,60},{14,62},{16,0},... | collective-permute-start | bytes 208904 | tf_op jit(solution)/shard_map/along_y/ppermute | solution.py:260
  37.2 7.3 %collective-permute-start.5 = (bf16[272,128]{1,0:T(8,128)(2,1)S(1)}, bf16[272,128]{1,0:T(8,128)(2,1)S(1)}, u32[]{:S(2)}, u32[]{:S(2)}) collective-permute-start(bf16[272,128]{1,0:T(8,128)(2,1)S(1)} %plane_total.1.own_ref), channel_id=1, source_target_pairs={{0,128},{2,130},{4,132},{6,134},{8,136},{10,138},{12,140},{14,142}... | collective-permute-start | bytes 208904 | tf_op jit(solution)/shard_map/along_x/ppermute | solution.py:260
  40.0 4.5 %collective-permute-start.4 = (bf16[272,128]{1,0:T(8,128)(2,1)S(1)}, bf16[272,128]{1,0:T(8,128)(2,1)S(1)}, u32[]{:S(2)}, u32[]{:S(2)}) collective-permute-start(bf16[272,128]{1,0:T(8,128)(2,1)S(1)} %plane_total.1.own_ref), channel_id=1, source_target_pairs={{0,64},{2,66},{4,68},{6,70},{8,72},{10,74},{12,76},{14,78},{16,80}... | collective-permute-start | bytes 208904 | tf_op jit(solution)/shard_map/along_x/ppermute | solution.py:260
  40.3 4.1 %collective-permute-start.3 = (bf16[272,128]{1,0:T(8,128)(2,1)S(1)}, bf16[272,128]{1,0:T(8,128)(2,1)S(1)}, u32[]{:S(2)}, u32[]{:S(2)}) collective-permute-start(bf16[272,128]{1,0:T(8,128)(2,1)S(1)} %plane_total.1.own_ref), channel_id=1, source_target_pairs={{0,192},{2,194},{4,196},{6,198},{8,200},{10,202},{12,204},{14,206}... | collective-permute-start | bytes 208904 | tf_op jit(solution)/shard_map/along_x/ppermute | solution.py:260
  44.5 13.0 %copy-start.2 = (bf16[2,8,128,128]{3,2,1,0:T(8,128)(2,1)S(1)}, bf16[2,8,128,128]{3,2,1,0:T(8,128)(2,1)}, u32[]{:S(2)}) copy-start(bf16[2,8,128,128]{3,2,1,0:T(8,128)(2,1)} %trans_ref.1) | copy-start | bytes 1572868
  44.5 13.0 %copy-start.3 = (bf16[128,1024]{1,0:T(8,128)(2,1)S(1)}, bf16[128,1024]{1,0:T(8,128)(2,1)}, u32[]{:S(2)}) copy-start(bf16[128,1024]{1,0:T(8,128)(2,1)} %query_ref.3) | copy-start | bytes 786436
  45.1 12.3 %copy-start = (bf16[128,1024]{1,0:T(8,128)(2,1)S(1)}, bf16[128,1024]{1,0:T(8,128)(2,1)}, u32[]{:S(2)}) copy-start(bf16[128,1024]{1,0:T(8,128)(2,1)} %key_ref.3) | copy-start | bytes 786436
  45.1 12.3 %copy-start.1 = (bf16[128,1024]{1,0:T(8,128)(2,1)S(1)}, bf16[128,1024]{1,0:T(8,128)(2,1)}, u32[]{:S(2)}) copy-start(bf16[128,1024]{1,0:T(8,128)(2,1)} %value_ref.3) | copy-start | bytes 786436
  59.0 6.7 %collective-permute-start.6 = (bf16[64,1024]{1,0:T(8,128)(2,1)S(1)}, bf16[64,1024]{1,0:T(8,128)(2,1)S(1)}, u32[]{:S(2)}, u32[]{:S(2)}) collective-permute-start(bf16[64,1024]{1,0:T(8,128)(2,1)S(1)} %get-tuple-element.24), channel_id=1, source_target_pairs={{0,1},{1,0},{2,3},{3,2},{4,5},{5,4},{6,7},{7,6},{8,9},{9,8},{10,11... | collective-permute-start | bytes 393224 | tf_op jit(solution)/shard_map/to_tokens/ppermute | solution.py:298

commit v3 on v2

--- a/solution.py
+++ b/solution.py
@@ -12,7 +12,6 @@
 BF16 = jnp.bfloat16
 VMEM = pl.BlockSpec(memory_space=pltpu.VMEM)
 PLAIN = pl.BlockSpec(memory_space=pltpu.VMEM)
-SMEM = pl.BlockSpec(memory_space=pltpu.SMEM)
 ANY = pl.BlockSpec(memory_space=pl.ANY)
 
 
@@ -70,41 +69,36 @@
 
 
 def local_compose(
-    trans_hbm, gate_ref, key_hbm, value_hbm, wire_ref, trans_ref, key_ref, value_ref, sems
+    trans_hbm, gate_hbm, key_hbm, value_hbm, wire_ref, trans_ref, gate_ref, key_ref, value_ref, sems
 ):
     heads = range(trans_ref.shape[1])
     rows = key_ref.shape[0] // 2
     pairs = (
+        (gate_hbm, gate_ref),
         (key_hbm, key_ref),
         (value_hbm, value_ref),
-        (trans_hbm.at[1], trans_ref.at[1]),
-        (trans_hbm.at[0], trans_ref.at[0]),
+        (trans_hbm, trans_ref),
     )
     copies = [pltpu.make_async_copy(*pair, sems.at[i]) for i, pair in enumerate(pairs)]
     for copy in copies:
         copy.start()
     eye = eye_mask()
-    copies[0].wait()
     copies[1].wait()
+    copies[2].wait()
 
     def update(c, h):
         here = (pl.ds(c * rows, rows), pl.ds(h * D, D))
         return dot(value_ref[here], key_ref[here], 0, 0)
 
-    updates = [(update(0, h), update(1, h)) for h in heads]
-    copies[2].wait()
-    states = []
-    for h in heads:
-        upd0, upd1 = updates[h]
-        high = upd0.astype(BF16)
-        low = (upd0 - high.astype(F32)).astype(BF16)
-        moved = dot(jnp.concatenate([high, low], axis=0), trans_ref[1, h], 1, 1)
-        states.append(gate_ref[1, h] * (moved[:D] + moved[D:]) + upd1)
+    updates = [(update(0, h).astype(BF16), update(1, h)) for h in heads]
+    copies[0].wait()
     copies[3].wait()
     for h in heads:
-        matrix = dot(trans_ref[0, h], trans_ref[1, h], 0, 1)
-        matrix = (gate_ref[0, h] * gate_ref[1, h]) * matrix
-        pack(wire_ref, (h,), jnp.concatenate([matrix, states[h]], axis=0), eye)
+        first, second = updates[h]
+        a1 = trans_ref[1, h]
+        state = gate_ref[1, h] * dot(first, a1, 1, 1) + second
+        matrix = (gate_ref[0, h] * gate_ref[1, h]) * dot(trans_ref[0, h], a1, 0, 1)
+        pack(wire_ref, (h,), jnp.concatenate([matrix, state], axis=0), eye)
 
 
 def line_total(wire_ref, total_ref):
@@ -119,8 +113,10 @@
     pack(total_ref, (), runs[0], eye)
 
 
-def line_before(wire_ref, gain_in_ref, pre_ref, gain_ref):
+def line_before(wire_ref, gain_in_ref, gate_in_ref, pre_ref, gain_ref, gate_ref):
     gain_ref[...] = gain_in_ref[...]
+    for h in range(gate_ref.shape[0]):
+        gate_ref[pl.ds(h, 1)] = jnp.broadcast_to(gate_in_ref[0:1, h : h + 1], (1, D))
     eye = eye_mask()
     run = jnp.concatenate([eye.astype(F32), jnp.zeros((D, D), F32)], axis=0)
     for z in range(wire_ref.shape[0]):
@@ -133,7 +129,7 @@
 
 def sort_ring(stride, refs, sorted_ref):
     me = lax.rem(lax.axis_index("seq") // stride, 4)
-    for d, ref in zip((0, 3, 1, 2), refs):
+    for d, ref in zip((0, 2, 1, 3), refs):
         sorted_ref[lax.rem(me + 4 - d, 4)] = ref[...]
     return me
 
@@ -200,7 +196,7 @@
         cols = pl.ds(h * D, D)
         entering = state_ref[h]
         upd = dot(value_ref[pl.ds(0, rows), cols], key_ref[pl.ds(0, rows), cols], 0, 0)
-        later = gate_ref[0, h] * dot(entering, trans_ref[0, h], 1, 1) + upd
+        later = gate_ref[pl.ds(h, 1)] * dot(entering, trans_ref[0, h], 1, 1) + upd
         first = entering.astype(F32)
         used_ref[h] = jnp.where(me == 0, later, first).astype(BF16)
         kept_ref[h] = jnp.where(me == 0, first, later).astype(BF16)
@@ -211,14 +207,18 @@
     normed_block(1 - me, query_ref, key_ref, value_ref, used_ref, gain_ref, write)
 
 
-def kept_outputs(query_ref, key_ref, value_ref, state_ref, gain_ref, out_ref):
+def kept_outputs(query_ref, key_ref, value_ref, state_ref, gain_ref, out_hbm, half_ref, sem):
     me = lax.axis_index("head")
-    start = me * (state_ref.shape[0] * D)
+    width = half_ref.shape[1]
 
     def write(h, value):
-        out_ref[:, pl.ds(pl.multiple_of(start + h * D, D), D)] = value
+        half_ref[:, pl.ds(h * D, D)] = value
 
     normed_block(me, query_ref, key_ref, value_ref, state_ref, gain_ref, write)
+    here = pl.ds(pl.multiple_of(me * width, width), width)
+    copy = pltpu.make_async_copy(half_ref, out_hbm.at[:, here], sem)
+    copy.start()
+    copy.wait()
 
 
 def call(kernel, outs, *operands, scratch=(), flops=0, specs=None):
@@ -234,7 +234,7 @@
         kernel,
         out_shape=shapes,
         in_specs=specs,
-        out_specs=[VMEM] * len(outs),
+        out_specs=[ANY if len(out) > 2 else VMEM for out in outs],
         scratch_shapes=scratch,
         cost_estimate=pl.CostEstimate(flops=flops, bytes_accessed=1 << 20, transcendentals=0),
         name=kernel.__name__,
@@ -252,7 +252,7 @@
 
     def around(total, stride):
         out = []
-        for d in (3, 1, 2):
+        for d in (2, 1, 3):
             pairs = []
             for s in range(count):
                 at = s // stride % 4
@@ -261,9 +261,10 @@
         return lax.optimization_barrier(out)
 
     (wire,) = call(
-        local_compose, [line], transitions, gates, keys, values, specs=[ANY, SMEM, ANY, ANY],
+        local_compose, [line], transitions, gates, keys, values, specs=[ANY] * 4,
         scratch=[
             pltpu.VMEM(transitions.shape, BF16),
+            pltpu.SMEM(gates.shape, F32),
             pltpu.VMEM(keys.shape, BF16),
             pltpu.VMEM(values.shape, BF16),
             pltpu.SemaphoreType.DMA((4,)),
@@ -274,8 +275,9 @@
     (total,) = call(line_total, [one], wire)
     with jax.named_scope("along_y"):
         others = around(total, 8)
-    line_pre, gain = call(
-        line_before, [line, ((1, D), F32)], wire, norm_gain.reshape(1, D), specs=[VMEM, PLAIN]
+    line_pre, gain, gate = call(
+        line_before, [line, ((1, D), F32), ((heads, D), F32)],
+        wire, norm_gain.reshape(1, D), gates, specs=[VMEM, PLAIN, PLAIN],
     )
     (whole,) = call(plane_total, [one], total, *others, scratch=ring)
     with jax.named_scope("along_x"):
@@ -290,8 +292,7 @@
     send, kept = call(
         sent_outputs,
         [(half, BF16), ((heads, D, D), BF16)],
-        queries, keys, values, transitions, gates, states, gain,
-        specs=[VMEM] * 4 + [SMEM] + [VMEM] * 2,
+        queries, keys, values, transitions, gate, states, gain,
         scratch=[pltpu.VMEM((heads, D, D), BF16)],
     )
     with jax.named_scope("to_tokens"):
@@ -299,6 +300,7 @@
     (out,) = call(
         kept_outputs, [((tokens // 2, 2 * heads * D), BF16, "hbm")],
         queries, keys, values, kept, gain,
+        scratch=[pltpu.VMEM(half, BF16), pltpu.SemaphoreType.DMA(())],
     )
     there = (1 - lax.axis_index("head")) * (heads * D)
     return lax.dynamic_update_slice(out, other, (0, there))

time: 66.5 us -> 64.9 us (0.976)
  Pallas kernels: 8.77 us -> 7.21 us
    pallas_call x8, Pallas kernels: 8.77 us -> 7.21 us  [call(): pl.pallas_call(kernel, out_shape=shapes, in_specs=specs, out_specs=[ANY i...]
where the time goes in v3:
time: 64.9 us; the launch traced here: 64.7 us
  blocking collectives  37.5 us (58%)
  starting transfers between devices  16.6 us (26%)
  Pallas kernels  7.21 us (11%)
  waiting for transfers between devices  2.54 us (4%)
  local copies, waits for them, and re-layouts  0.7 us (1%)
    all_to_all x1, blocking collectives, shards(): lax.all_to_all(wire, 'seq', 0, 0, axis_index_groups=lines, tiled=True)  25.3 us
    all_to_all x1, blocking collectives, shards(): lax.all_to_all(states, 'seq', 0, 0, axis_index_groups=lines, tiled=True)  12.3 us
    ppermute x6, starting transfers between devices, around(): out.append(lax.ppermute(total, 'seq', pairs))  11.2 us
    pallas_call x8, Pallas kernels, call(): pl.pallas_call(kernel, out_shape=shapes, in_specs=specs, out_specs=[ANY i...  7.21 us
    ppermute x1, starting transfers between devices, shards(): other = lax.ppermute(send, 'head', [(0, 1), (1, 0)])  5.4 us
    ppermute x6, waiting for transfers between devices, around(): out.append(lax.ppermute(total, 'seq', pairs))  2.54 us
  transfers between devices with their start and end apart: 7, of which 1 were waited for; matrix products, arithmetic and copies ran while one was open for 0% of the time, Pallas kernels for 5%

profile of v3, /device:TPU:1, one launch (start us, length us, event | category | flops | bytes accessed | tf_op | source)
XLA Modules:
  0.0 64.7 jit_solution(7031825341050380610)
XLA Ops:
  0.0 1.9 %local_compose.1 = bf16[8,272,128]{2,1,0:T(8,128)(2,1)S(1)} custom-call(bf16[2,8,128,128]{3,2,1,0:T(8,128)(2,1)} %trans_ref.1, f32[2,8]{1,0:T(2,128)} %gate_in_ref.1, bf16[128,1024]{1,0:T(8,128)(2,1)} %key_ref.3, bf16[128,1024]{1,0:T(8,128)(2,1)} %value_ref.3), custom_call_target="tpu_custom_call" | custom-call | bytes 1048576 | tf_op jit(solution)/shard_map/local_compose/pallas_call | solution.py:233
  1.9 25.3 %all_to_all.10.wire_ref = bf16[8,272,128]{2,1,0:T(8,128)(2,1)S(1)} all-to-all(bf16[8,272,128]{2,1,0:T(8,128)(2,1)S(1)} %local_compose.1), channel_id=1, replica_groups={{0,2,4,6,8,10,12,14},{16,18,20,22,24,26,28,30},{32,34,36,38,40,42,44,46..., dimensions={0} | all-to-all | bytes 1114112 | tf_op jit(solution)/shard_map/to_owners/all_to_all | solution.py:274
  27.1 0.5 line_total.1.own_ref
  27.7 3.0 %collective-permute-start = (bf16[272,128]{1,0:T(8,128)(2,1)S(1)}, bf16[272,128]{1,0:T(8,128)(2,1)S(1)}, u32[]{:S(2)}, u32[]{:S(2)}) collective-permute-start(bf16[272,128]{1,0:T(8,128)(2,1)S(1)} %line_total.1.own_ref), channel_id=1, source_target_pairs={{0,32},{2,34},{4,36},{6,38},{8,40},{10,42},{12,44},{14,46},{16,48}... | collective-permute-start | bytes 208904 | tf_op jit(solution)/shard_map/along_y/ppermute | solution.py:260
  30.7 0.4 collective-permute-start.1
  31.1 2.3 %collective-permute-start.2 = (bf16[272,128]{1,0:T(8,128)(2,1)S(1)}, bf16[272,128]{1,0:T(8,128)(2,1)S(1)}, u32[]{:S(2)}, u32[]{:S(2)}) collective-permute-start(bf16[272,128]{1,0:T(8,128)(2,1)S(1)} %line_total.1.own_ref), channel_id=1, source_target_pairs={{0,48},{2,50},{4,52},{6,54},{8,56},{10,58},{12,60},{14,62},{16,0},... | collective-permute-start | bytes 208904 | tf_op jit(solution)/shard_map/along_y/ppermute | solution.py:260
  33.4 0.0 collective-permute-done.a_ref
  33.4 2.5 %collective-permute-done.1.b_ref = bf16[272,128]{1,0:T(8,128)(2,1)S(1)} collective-permute-done((bf16[272,128]{1,0:T(8,128)(2,1)S(1)}, bf16[272,128]{1,0:T(8,128)(2,1)S(1)}, u32[]{:S(2)}, u32[]{:S(2)}) %collective-permute-start.1) | collective-permute-done | bytes 69664 | tf_op jit(solution)/shard_map/along_y/ppermute | solution.py:260
  35.9 0.0 collective-permute-done.2.c_ref
  35.9 0.4 plane_total.1.own_ref
  36.3 2.8 %collective-permute-start.3 = (bf16[272,128]{1,0:T(8,128)(2,1)S(1)}, bf16[272,128]{1,0:T(8,128)(2,1)S(1)}, u32[]{:S(2)}, u32[]{:S(2)}) collective-permute-start(bf16[272,128]{1,0:T(8,128)(2,1)S(1)} %plane_total.1.own_ref), channel_id=1, source_target_pairs={{0,128},{2,130},{4,132},{6,134},{8,136},{10,138},{12,140},{14,142}... | collective-permute-start | bytes 208904 | tf_op jit(solution)/shard_map/along_x/ppermute | solution.py:260
  39.1 0.3 collective-permute-start.4
  39.4 2.4 %collective-permute-start.5 = (bf16[272,128]{1,0:T(8,128)(2,1)S(1)}, bf16[272,128]{1,0:T(8,128)(2,1)S(1)}, u32[]{:S(2)}, u32[]{:S(2)}) collective-permute-start(bf16[272,128]{1,0:T(8,128)(2,1)S(1)} %plane_total.1.own_ref), channel_id=1, source_target_pairs={{0,192},{2,194},{4,196},{6,198},{8,200},{10,202},{12,204},{14,206}... | collective-permute-start | bytes 208904 | tf_op jit(solution)/shard_map/along_x/ppermute | solution.py:260
  41.8 1.5 %line_before.1 = (bf16[8,272,128]{2,1,0:T(8,128)(2,1)S(1)}, f32[1,128]{1,0:T(1,128)S(1)}, f32[8,128]{1,0:T(8,128)S(1)}) custom-call(bf16[8,272,128]{2,1,0:T(8,128)(2,1)S(1)} %all_to_all.10.wire_ref, f32[1,128]{1,0:T(1,128)} %bitcast.1, f32[2,8]{1,0:T(2,128)} %gate_in_ref.1), custom_call_target="tpu_custom_call" | custom-call | bytes 1048576 | tf_op jit(solution)/shard_map/line_before/pallas_call | solution.py:233
  43.2 0.3 plane_before.1.plane_ref
  43.6 0.0 collective-permute-done.3.a_ref
  43.6 0.0 collective-permute-done.4.b_ref
  43.6 0.0 collective-permute-done.5.c_ref
  43.6 0.0 copy-start.2
  43.6 0.0 copy-start.3
  43.6 0.6 enter_states.1
  44.3 0.0 copy-start
  44.3 0.0 copy-start.1
  44.3 12.3 %all_to_all.11.state_ref = bf16[8,128,128]{2,1,0:T(8,128)(2,1)S(1)} all-to-all(bf16[8,128,128]{2,1,0:T(8,128)(2,1)S(1)} %enter_states.1), channel_id=1, replica_groups={{0,2,4,6,8,10,12,14},{16,18,20,22,24,26,28,30},{32,34,36,38,40,42,44,46..., dimensions={0} | all-to-all | bytes 524288 | tf_op jit(solution)/shard_map/from_owners/all_to_all | solution.py:290
  56.6 0.0 copy-done.2
  56.6 0.0 copy-done.3
  56.6 0.0 copy-done
  56.6 0.0 copy-done.1
  56.6 0.8 %sent_outputs.1 = (bf16[64,1024]{1,0:T(8,128)(2,1)S(1)}, bf16[8,128,128]{2,1,0:T(8,128)(2,1)S(1)}) custom-call(bf16[128,1024]{1,0:T(8,128)(2,1)S(1)} %copy-done.3, bf16[128,1024]{1,0:T(8,128)(2,1)S(1)} %copy-done, bf16[128,1024]{1,0:T(8,128)(2,1)S(1)} %copy-done.1, bf16[2,8,128,128]{3,2,1,0:T(8,128)(2,1)S(1)} %copy-done.2, ...), custom_call_target="tpu_custom_call" | custom-call | bytes 1048576 | tf_op jit(solution)/shard_map/sent_outputs/pallas_call | solution.py:233
  57.4 5.4 %collective-permute-start.6 = (bf16[64,1024]{1,0:T(8,128)(2,1)S(1)}, bf16[64,1024]{1,0:T(8,128)(2,1)S(1)}, u32[]{:S(2)}, u32[]{:S(2)}) collective-permute-start(bf16[64,1024]{1,0:T(8,128)(2,1)S(1)} %get-tuple-element.26), channel_id=1, source_target_pairs={{0,1},{1,0},{2,3},{3,2},{4,5},{5,4},{6,7},{7,6},{8,9},{9,8},{10,11... | collective-permute-start | bytes 393224 | tf_op jit(solution)/shard_map/to_tokens/ppermute | solution.py:299
  62.8 1.2 %kept_outputs.1 = bf16[64,2048]{1,0:T(8,128)(2,1)} custom-call(bf16[128,1024]{1,0:T(8,128)(2,1)S(1)} %copy-done.3, bf16[128,1024]{1,0:T(8,128)(2,1)S(1)} %copy-done, bf16[128,1024]{1,0:T(8,128)(2,1)S(1)} %copy-done.1, bf16[8,128,128]{2,1,0:T(8,128)(2,1)S(1)} %get-tuple-element.25.state_ref, f32[1,128]{1,0:T(1,128)S(1)} %get-tuple-element.24.gain_ref), custom_call_target="tpu_custom_call" | custom-call | bytes 1048576 | tf_op jit(solution)/shard_map/kept_outputs/pallas_call | solution.py:233
  64.0 0.0 collective-permute-done.6
  64.0 0.7 %constant_dynamic-update-slice_fusion = bf16[64,2048]{1,0:T(8,128)(2,1)} fusion(bf16[64,2048]{1,0:T(8,128)(2,1)} %kept_outputs.1, bf16[64,1024]{1,0:T(8,128)(2,1)S(1)} %collective-permute-done.6, s32[]{:T(128)S(6)} %select_n.3), kind=kLoop, calls=%fused_computation | loop fusion | bytes 262148 | tf_op jit(solution)/shard_map/dynamic_update_slice | solution.py:306
Async XLA Ops:
  27.7 5.7 %collective-permute-start = (bf16[272,128]{1,0:T(8,128)(2,1)S(1)}, bf16[272,128]{1,0:T(8,128)(2,1)S(1)}, u32[]{:S(2)}, u32[]{:S(2)}) collective-permute-start(bf16[272,128]{1,0:T(8,128)(2,1)S(1)} %line_total.1.own_ref), channel_id=1, source_target_pairs={{0,32},{2,34},{4,36},{6,38},{8,40},{10,42},{12,44},{14,46},{16,48}... | collective-permute-start | bytes 208904 | tf_op jit(solution)/shard_map/along_y/ppermute | solution.py:260
  30.7 5.2 %collective-permute-start.1 = (bf16[272,128]{1,0:T(8,128)(2,1)S(1)}, bf16[272,128]{1,0:T(8,128)(2,1)S(1)}, u32[]{:S(2)}, u32[]{:S(2)}) collective-permute-start(bf16[272,128]{1,0:T(8,128)(2,1)S(1)} %line_total.1.own_ref), channel_id=1, source_target_pairs={{0,16},{2,18},{4,20},{6,22},{8,24},{10,26},{12,28},{14,30},{16,32}... | collective-permute-start | bytes 208904 | tf_op jit(solution)/shard_map/along_y/ppermute | solution.py:260
  31.1 4.8 %collective-permute-start.2 = (bf16[272,128]{1,0:T(8,128)(2,1)S(1)}, bf16[272,128]{1,0:T(8,128)(2,1)S(1)}, u32[]{:S(2)}, u32[]{:S(2)}) collective-permute-start(bf16[272,128]{1,0:T(8,128)(2,1)S(1)} %line_total.1.own_ref), channel_id=1, source_target_pairs={{0,48},{2,50},{4,52},{6,54},{8,56},{10,58},{12,60},{14,62},{16,0},... | collective-permute-start | bytes 208904 | tf_op jit(solution)/shard_map/along_y/ppermute | solution.py:260
  36.3 7.3 %collective-permute-start.3 = (bf16[272,128]{1,0:T(8,128)(2,1)S(1)}, bf16[272,128]{1,0:T(8,128)(2,1)S(1)}, u32[]{:S(2)}, u32[]{:S(2)}) collective-permute-start(bf16[272,128]{1,0:T(8,128)(2,1)S(1)} %plane_total.1.own_ref), channel_id=1, source_target_pairs={{0,128},{2,130},{4,132},{6,134},{8,136},{10,138},{12,140},{14,142}... | collective-permute-start | bytes 208904 | tf_op jit(solution)/shard_map/along_x/ppermute | solution.py:260
  39.1 4.5 %collective-permute-start.4 = (bf16[272,128]{1,0:T(8,128)(2,1)S(1)}, bf16[272,128]{1,0:T(8,128)(2,1)S(1)}, u32[]{:S(2)}, u32[]{:S(2)}) collective-permute-start(bf16[272,128]{1,0:T(8,128)(2,1)S(1)} %plane_total.1.own_ref), channel_id=1, source_target_pairs={{0,64},{2,66},{4,68},{6,70},{8,72},{10,74},{12,76},{14,78},{16,80}... | collective-permute-start | bytes 208904 | tf_op jit(solution)/shard_map/along_x/ppermute | solution.py:260
  39.4 4.2 %collective-permute-start.5 = (bf16[272,128]{1,0:T(8,128)(2,1)S(1)}, bf16[272,128]{1,0:T(8,128)(2,1)S(1)}, u32[]{:S(2)}, u32[]{:S(2)}) collective-permute-start(bf16[272,128]{1,0:T(8,128)(2,1)S(1)} %plane_total.1.own_ref), channel_id=1, source_target_pairs={{0,192},{2,194},{4,196},{6,198},{8,200},{10,202},{12,204},{14,206}... | collective-permute-start | bytes 208904 | tf_op jit(solution)/shard_map/along_x/ppermute | solution.py:260
  43.6 13.0 %copy-start.2 = (bf16[2,8,128,128]{3,2,1,0:T(8,128)(2,1)S(1)}, bf16[2,8,128,128]{3,2,1,0:T(8,128)(2,1)}, u32[]{:S(2)}) copy-start(bf16[2,8,128,128]{3,2,1,0:T(8,128)(2,1)} %trans_ref.1) | copy-start | bytes 1572868
  43.6 12.9 %copy-start.3 = (bf16[128,1024]{1,0:T(8,128)(2,1)S(1)}, bf16[128,1024]{1,0:T(8,128)(2,1)}, u32[]{:S(2)}) copy-start(bf16[128,1024]{1,0:T(8,128)(2,1)} %query_ref.3) | copy-start | bytes 786436
  44.3 12.3 %copy-start = (bf16[128,1024]{1,0:T(8,128)(2,1)S(1)}, bf16[128,1024]{1,0:T(8,128)(2,1)}, u32[]{:S(2)}) copy-start(bf16[128,1024]{1,0:T(8,128)(2,1)} %key_ref.3) | copy-start | bytes 786436
  44.3 12.3 %copy-start.1 = (bf16[128,1024]{1,0:T(8,128)(2,1)S(1)}, bf16[128,1024]{1,0:T(8,128)(2,1)}, u32[]{:S(2)}) copy-start(bf16[128,1024]{1,0:T(8,128)(2,1)} %value_ref.3) | copy-start | bytes 786436
  57.4 6.6 %collective-permute-start.6 = (bf16[64,1024]{1,0:T(8,128)(2,1)S(1)}, bf16[64,1024]{1,0:T(8,128)(2,1)S(1)}, u32[]{:S(2)}, u32[]{:S(2)}) collective-permute-start(bf16[64,1024]{1,0:T(8,128)(2,1)S(1)} %get-tuple-element.26), channel_id=1, source_target_pairs={{0,1},{1,0},{2,3},{3,2},{4,5},{5,4},{6,7},{7,6},{8,9},{9,8},{10,11... | collective-permute-start | bytes 393224 | tf_op jit(solution)/shard_map/to_tokens/ppermute | solution.py:299

commit v4 on v3

--- a/solution.py
+++ b/solution.py
@@ -7,7 +7,8 @@
 
 EPS = 1e-06
 D = 128
-ROWS = 2 * D + 16
+ROWS = 2 * D
+SCALE = 2.0**60
 F32 = jnp.float32
 BF16 = jnp.bfloat16
 VMEM = pl.BlockSpec(memory_space=pltpu.VMEM)
@@ -31,21 +32,26 @@
     return row, jnp.where(eye, 0.0, matrix).astype(BF16)
 
 
+def code(row):
+    far = row * SCALE
+    far = jnp.where(row < 0.0, jnp.minimum(far, -2.0), jnp.maximum(far, 2.0))
+    return jnp.where((row >= 0.5) & (row <= 1.75), row - 1.0, far)
+
+
+def decode(row):
+    return jnp.where(jnp.abs(row) <= 1.0, row + 1.0, row * (1.0 / SCALE))
+
+
 def pack(ref, at, both, eye):
-    row, rest = split(both[:D], eye)
-    high = row.astype(BF16)
-    low = (row - high.astype(F32)).astype(BF16)
-    ref[(*at, pl.ds(0, D))] = rest
+    matrix = both[:D]
+    row = jnp.sum(jnp.where(eye, matrix, 0.0), axis=0, keepdims=True)
+    ref[(*at, pl.ds(0, D))] = jnp.where(eye, code(row), matrix).astype(BF16)
     ref[(*at, pl.ds(D, D))] = both[D:].astype(BF16)
-    place = lax.broadcasted_iota(jnp.int32, (16, D), 0)
-    tail = jnp.where(place == 0, high.astype(F32), jnp.where(place == 1, low.astype(F32), 0.0))
-    ref[(*at, pl.ds(2 * D, 16))] = tail.astype(BF16)
 
 
 def unpack(ref, at=()):
-    tail = ref[(*at, pl.ds(2 * D, 16))].astype(F32)
-    rest = ref[(*at, pl.ds(0, D))]
-    return tail[0:1] + tail[1:2], rest, ref[(*at, pl.ds(D, D))].astype(F32)
+    row, rest = split(ref[(*at, pl.ds(0, D))], eye_mask())
+    return decode(row), rest, ref[(*at, pl.ds(D, D))].astype(F32)
 
 
 def dense(parts, eye):
@@ -129,8 +135,8 @@
 
 def sort_ring(stride, refs, sorted_ref):
     me = lax.rem(lax.axis_index("seq") // stride, 4)
-    for d, ref in zip((0, 2, 1, 3), refs):
-        sorted_ref[lax.rem(me + 4 - d, 4)] = ref[...]
+    for d, ref in zip((0, 2, 3, 1), refs):
+        sorted_ref[me ^ d] = ref[...]
     return me
 
 
@@ -252,11 +258,11 @@
 
     def around(total, stride):
         out = []
-        for d in (2, 1, 3):
+        for d in (2, 3, 1):
             pairs = []
             for s in range(count):
                 at = s // stride % 4
-                pairs.append((s, s + ((at + d) % 4 - at) * stride))
+                pairs.append((s, s + ((at ^ d) - at) * stride))
             out.append(lax.ppermute(total, "seq", pairs))
         return lax.optimization_barrier(out)
 

time: 64.9 us -> 64.1 us (0.988)
  starting transfers between devices: 16.6 us -> 12.9 us
  waiting for transfers between devices: 2.54 us -> 5.85 us
    ppermute x6, starting transfers between devices: 11.2 us -> 7.49 us  [around(): out.append(lax.ppermute(total, 'seq', pairs))]
    ppermute x6, waiting for transfers between devices: 2.54 us -> 5.85 us  [around(): out.append(lax.ppermute(total, 'seq', pairs))]
  transfers between devices with their start and end apart: 7 -> 7, of which waited for: 1 -> 3; matrix products, arithmetic and copies ran while one was open for 0% -> 0% of each run, Pallas kernels for 5% -> 5%
where the time goes in v4:
time: 64.1 us; the launch traced here: 64 us
  blocking collectives  37.1 us (58%)
  starting transfers between devices  12.9 us (20%)
  Pallas kernels  7.32 us (11%)
  waiting for transfers between devices  5.85 us (9%)
  local copies, waits for them, and re-layouts  0.69 us (1%)
    all_to_all x1, blocking collectives, shards(): lax.all_to_all(wire, 'seq', 0, 0, axis_index_groups=lines, tiled=True)  24.8 us
    all_to_all x1, blocking collectives, shards(): lax.all_to_all(states, 'seq', 0, 0, axis_index_groups=lines, tiled=True)  12.3 us
    ppermute x6, starting transfers between devices, around(): out.append(lax.ppermute(total, 'seq', pairs))  7.49 us
    pallas_call x8, Pallas kernels, call(): pl.pallas_call(kernel, out_shape=shapes, in_specs=specs, out_specs=[ANY i...  7.32 us
    ppermute x6, waiting for transfers between devices, around(): out.append(lax.ppermute(total, 'seq', pairs))  5.85 us
    ppermute x1, starting transfers between devices, shards(): other = lax.ppermute(send, 'head', [(0, 1), (1, 0)])  5.41 us
  transfers between devices with their start and end apart: 7, of which 3 were waited for; matrix products, arithmetic and copies ran while one was open for 0% of the time, Pallas kernels for 5%

profile of v4, /device:TPU:1, one launch (start us, length us, event | category | flops | bytes accessed | tf_op | source)
XLA Modules:
  0.0 64.0 jit_solution(5618675600568893493)
XLA Ops:
  0.0 1.9 %local_compose.1 = bf16[8,256,128]{2,1,0:T(8,128)(2,1)S(1)} custom-call(bf16[2,8,128,128]{3,2,1,0:T(8,128)(2,1)} %trans_ref.1, f32[2,8]{1,0:T(2,128)} %gate_in_ref.1, bf16[128,1024]{1,0:T(8,128)(2,1)} %key_ref.3, bf16[128,1024]{1,0:T(8,128)(2,1)} %value_ref.3), custom_call_target="tpu_custom_call" | custom-call | bytes 1048576 | tf_op jit(solution)/shard_map/local_compose/pallas_call | solution.py:239
  1.9 24.8 %all_to_all.10.wire_ref = bf16[8,256,128]{2,1,0:T(8,128)(2,1)S(1)} all-to-all(bf16[8,256,128]{2,1,0:T(8,128)(2,1)S(1)} %local_compose.1), channel_id=1, replica_groups={{0,2,4,6,8,10,12,14},{16,18,20,22,24,26,28,30},{32,34,36,38,40,42,44,46..., dimensions={0} | all-to-all | bytes 1048576 | tf_op jit(solution)/shard_map/to_owners/all_to_all | solution.py:280
  26.7 0.6 line_total.1.own_ref
  27.2 3.0 %collective-permute-start = (bf16[256,128]{1,0:T(8,128)(2,1)S(1)}, bf16[256,128]{1,0:T(8,128)(2,1)S(1)}, u32[]{:S(2)}, u32[]{:S(2)}) collective-permute-start(bf16[256,128]{1,0:T(8,128)(2,1)S(1)} %line_total.1.own_ref), channel_id=1, source_target_pairs={{0,32},{2,34},{4,36},{6,38},{8,40},{10,42},{12,44},{14,46},{16,48}... | collective-permute-start | bytes 196616 | tf_op jit(solution)/shard_map/along_y/ppermute | solution.py:266
  30.2 0.8 %collective-permute-start.1 = (bf16[256,128]{1,0:T(8,128)(2,1)S(1)}, bf16[256,128]{1,0:T(8,128)(2,1)S(1)}, u32[]{:S(2)}, u32[]{:S(2)}) collective-permute-start(bf16[256,128]{1,0:T(8,128)(2,1)S(1)} %line_total.1.own_ref), channel_id=1, source_target_pairs={{0,48},{2,50},{4,52},{6,54},{8,56},{10,58},{12,60},{14,62},{16,32}... | collective-permute-start | bytes 196616 | tf_op jit(solution)/shard_map/along_y/ppermute | solution.py:266
  31.0 0.0 collective-permute-start.2
  31.0 0.9 %collective-permute-done.a_ref = bf16[256,128]{1,0:T(8,128)(2,1)S(1)} collective-permute-done((bf16[256,128]{1,0:T(8,128)(2,1)S(1)}, bf16[256,128]{1,0:T(8,128)(2,1)S(1)}, u32[]{:S(2)}, u32[]{:S(2)}) %collective-permute-start) | collective-permute-done | bytes 65568 | tf_op jit(solution)/shard_map/along_y/ppermute | solution.py:266
  31.9 3.3 %collective-permute-done.1.b_ref = bf16[256,128]{1,0:T(8,128)(2,1)S(1)} collective-permute-done((bf16[256,128]{1,0:T(8,128)(2,1)S(1)}, bf16[256,128]{1,0:T(8,128)(2,1)S(1)}, u32[]{:S(2)}, u32[]{:S(2)}) %collective-permute-start.1) | collective-permute-done | bytes 65568 | tf_op jit(solution)/shard_map/along_y/ppermute | solution.py:266
  35.3 0.0 collective-permute-done.2.c_ref
  35.3 0.4 plane_total.1.own_ref
  35.7 2.8 %collective-permute-start.3 = (bf16[256,128]{1,0:T(8,128)(2,1)S(1)}, bf16[256,128]{1,0:T(8,128)(2,1)S(1)}, u32[]{:S(2)}, u32[]{:S(2)}) collective-permute-start(bf16[256,128]{1,0:T(8,128)(2,1)S(1)} %plane_total.1.own_ref), channel_id=1, source_target_pairs={{0,128},{2,130},{4,132},{6,134},{8,136},{10,138},{12,140},{14,142}... | collective-permute-start | bytes 196616 | tf_op jit(solution)/shard_map/along_x/ppermute | solution.py:266
  38.5 0.8 %collective-permute-start.4 = (bf16[256,128]{1,0:T(8,128)(2,1)S(1)}, bf16[256,128]{1,0:T(8,128)(2,1)S(1)}, u32[]{:S(2)}, u32[]{:S(2)}) collective-permute-start(bf16[256,128]{1,0:T(8,128)(2,1)S(1)} %plane_total.1.own_ref), channel_id=1, source_target_pairs={{0,192},{2,194},{4,196},{6,198},{8,200},{10,202},{12,204},{14,206}... | collective-permute-start | bytes 196616 | tf_op jit(solution)/shard_map/along_x/ppermute | solution.py:266
  39.4 0.0 collective-permute-start.5
  39.4 1.5 %line_before.1 = (bf16[8,256,128]{2,1,0:T(8,128)(2,1)S(1)}, f32[1,128]{1,0:T(1,128)S(1)}, f32[8,128]{1,0:T(8,128)S(1)}) custom-call(bf16[8,256,128]{2,1,0:T(8,128)(2,1)S(1)} %all_to_all.10.wire_ref, f32[1,128]{1,0:T(1,128)} %bitcast.1, f32[2,8]{1,0:T(2,128)} %gate_in_ref.1), custom_call_target="tpu_custom_call" | custom-call | bytes 1048576 | tf_op jit(solution)/shard_map/line_before/pallas_call | solution.py:239
  40.9 0.3 plane_before.1.plane_ref
  41.2 0.0 collective-permute-done.3.a_ref
  41.3 1.6 %collective-permute-done.4.b_ref = bf16[256,128]{1,0:T(8,128)(2,1)S(1)} collective-permute-done((bf16[256,128]{1,0:T(8,128)(2,1)S(1)}, bf16[256,128]{1,0:T(8,128)(2,1)S(1)}, u32[]{:S(2)}, u32[]{:S(2)}) %collective-permute-start.4) | collective-permute-done | bytes 65568 | tf_op jit(solution)/shard_map/along_x/ppermute | solution.py:266
  42.9 0.0 collective-permute-done.5.c_ref
  42.9 0.0 copy-start.2
  42.9 0.0 copy-start.3
  42.9 0.6 enter_states.1
  43.5 0.0 copy-start
  43.5 0.0 copy-start.1
  43.5 12.3 %all_to_all.11.state_ref = bf16[8,128,128]{2,1,0:T(8,128)(2,1)S(1)} all-to-all(bf16[8,128,128]{2,1,0:T(8,128)(2,1)S(1)} %enter_states.1), channel_id=1, replica_groups={{0,2,4,6,8,10,12,14},{16,18,20,22,24,26,28,30},{32,34,36,38,40,42,44,46..., dimensions={0} | all-to-all | bytes 524288 | tf_op jit(solution)/shard_map/from_owners/all_to_all | solution.py:296
  55.8 0.0 copy-done.2
  55.8 0.0 copy-done.3
  55.8 0.0 copy-done
  55.8 0.0 copy-done.1
  55.8 0.8 %sent_outputs.1 = (bf16[64,1024]{1,0:T(8,128)(2,1)S(1)}, bf16[8,128,128]{2,1,0:T(8,128)(2,1)S(1)}) custom-call(bf16[128,1024]{1,0:T(8,128)(2,1)S(1)} %copy-done.3, bf16[128,1024]{1,0:T(8,128)(2,1)S(1)} %copy-done, bf16[128,1024]{1,0:T(8,128)(2,1)S(1)} %copy-done.1, bf16[2,8,128,128]{3,2,1,0:T(8,128)(2,1)S(1)} %copy-done.2, ...), custom_call_target="tpu_custom_call" | custom-call | bytes 1048576 | tf_op jit(solution)/shard_map/sent_outputs/pallas_call | solution.py:239
  56.6 5.4 %collective-permute-start.6 = (bf16[64,1024]{1,0:T(8,128)(2,1)S(1)}, bf16[64,1024]{1,0:T(8,128)(2,1)S(1)}, u32[]{:S(2)}, u32[]{:S(2)}) collective-permute-start(bf16[64,1024]{1,0:T(8,128)(2,1)S(1)} %get-tuple-element.26), channel_id=1, source_target_pairs={{0,1},{1,0},{2,3},{3,2},{4,5},{5,4},{6,7},{7,6},{8,9},{9,8},{10,11... | collective-permute-start | bytes 393224 | tf_op jit(solution)/shard_map/to_tokens/ppermute | solution.py:305
  62.0 1.2 %kept_outputs.1 = bf16[64,2048]{1,0:T(8,128)(2,1)} custom-call(bf16[128,1024]{1,0:T(8,128)(2,1)S(1)} %copy-done.3, bf16[128,1024]{1,0:T(8,128)(2,1)S(1)} %copy-done, bf16[128,1024]{1,0:T(8,128)(2,1)S(1)} %copy-done.1, bf16[8,128,128]{2,1,0:T(8,128)(2,1)S(1)} %get-tuple-element.25.state_ref, f32[1,128]{1,0:T(1,128)S(1)} %get-tuple-element.24.gain_ref), custom_call_target="tpu_custom_call" | custom-call | bytes 1048576 | tf_op jit(solution)/shard_map/kept_outputs/pallas_call | solution.py:239
  63.3 0.0 collective-permute-done.6
  63.3 0.7 %constant_dynamic-update-slice_fusion = bf16[64,2048]{1,0:T(8,128)(2,1)} fusion(bf16[64,2048]{1,0:T(8,128)(2,1)} %kept_outputs.1, bf16[64,1024]{1,0:T(8,128)(2,1)S(1)} %collective-permute-done.6, s32[]{:T(128)S(6)} %select_n.3), kind=kLoop, calls=%fused_computation | loop fusion | bytes 262148 | tf_op jit(solution)/shard_map/dynamic_update_slice | solution.py:312
Async XLA Ops:
  27.2 4.7 %collective-permute-start = (bf16[256,128]{1,0:T(8,128)(2,1)S(1)}, bf16[256,128]{1,0:T(8,128)(2,1)S(1)}, u32[]{:S(2)}, u32[]{:S(2)}) collective-permute-start(bf16[256,128]{1,0:T(8,128)(2,1)S(1)} %line_total.1.own_ref), channel_id=1, source_target_pairs={{0,32},{2,34},{4,36},{6,38},{8,40},{10,42},{12,44},{14,46},{16,48}... | collective-permute-start | bytes 196616 | tf_op jit(solution)/shard_map/along_y/ppermute | solution.py:266
  30.2 5.0 %collective-permute-start.1 = (bf16[256,128]{1,0:T(8,128)(2,1)S(1)}, bf16[256,128]{1,0:T(8,128)(2,1)S(1)}, u32[]{:S(2)}, u32[]{:S(2)}) collective-permute-start(bf16[256,128]{1,0:T(8,128)(2,1)S(1)} %line_total.1.own_ref), channel_id=1, source_target_pairs={{0,48},{2,50},{4,52},{6,54},{8,56},{10,58},{12,60},{14,62},{16,32}... | collective-permute-start | bytes 196616 | tf_op jit(solution)/shard_map/along_y/ppermute | solution.py:266
  31.0 4.2 %collective-permute-start.2 = (bf16[256,128]{1,0:T(8,128)(2,1)S(1)}, bf16[256,128]{1,0:T(8,128)(2,1)S(1)}, u32[]{:S(2)}, u32[]{:S(2)}) collective-permute-start(bf16[256,128]{1,0:T(8,128)(2,1)S(1)} %line_total.1.own_ref), channel_id=1, source_target_pairs={{0,16},{2,18},{4,20},{6,22},{8,24},{10,26},{12,28},{14,30},{16,0},... | collective-permute-start | bytes 196616 | tf_op jit(solution)/shard_map/along_y/ppermute | solution.py:266
  35.7 5.6 %collective-permute-start.3 = (bf16[256,128]{1,0:T(8,128)(2,1)S(1)}, bf16[256,128]{1,0:T(8,128)(2,1)S(1)}, u32[]{:S(2)}, u32[]{:S(2)}) collective-permute-start(bf16[256,128]{1,0:T(8,128)(2,1)S(1)} %plane_total.1.own_ref), channel_id=1, source_target_pairs={{0,128},{2,130},{4,132},{6,134},{8,136},{10,138},{12,140},{14,142}... | collective-permute-start | bytes 196616 | tf_op jit(solution)/shard_map/along_x/ppermute | solution.py:266
  38.5 4.3 %collective-permute-start.4 = (bf16[256,128]{1,0:T(8,128)(2,1)S(1)}, bf16[256,128]{1,0:T(8,128)(2,1)S(1)}, u32[]{:S(2)}, u32[]{:S(2)}) collective-permute-start(bf16[256,128]{1,0:T(8,128)(2,1)S(1)} %plane_total.1.own_ref), channel_id=1, source_target_pairs={{0,192},{2,194},{4,196},{6,198},{8,200},{10,202},{12,204},{14,206}... | collective-permute-start | bytes 196616 | tf_op jit(solution)/shard_map/along_x/ppermute | solution.py:266
  39.4 3.5 %collective-permute-start.5 = (bf16[256,128]{1,0:T(8,128)(2,1)S(1)}, bf16[256,128]{1,0:T(8,128)(2,1)S(1)}, u32[]{:S(2)}, u32[]{:S(2)}) collective-permute-start(bf16[256,128]{1,0:T(8,128)(2,1)S(1)} %plane_total.1.own_ref), channel_id=1, source_target_pairs={{0,64},{2,66},{4,68},{6,70},{8,72},{10,74},{12,76},{14,78},{16,80}... | collective-permute-start | bytes 196616 | tf_op jit(solution)/shard_map/along_x/ppermute | solution.py:266
  42.9 13.0 %copy-start.2 = (bf16[2,8,128,128]{3,2,1,0:T(8,128)(2,1)S(1)}, bf16[2,8,128,128]{3,2,1,0:T(8,128)(2,1)}, u32[]{:S(2)}) copy-start(bf16[2,8,128,128]{3,2,1,0:T(8,128)(2,1)} %trans_ref.1) | copy-start | bytes 1572868
  42.9 13.0 %copy-start.3 = (bf16[128,1024]{1,0:T(8,128)(2,1)S(1)}, bf16[128,1024]{1,0:T(8,128)(2,1)}, u32[]{:S(2)}) copy-start(bf16[128,1024]{1,0:T(8,128)(2,1)} %query_ref.3) | copy-start | bytes 786436
  43.5 12.3 %copy-start = (bf16[128,1024]{1,0:T(8,128)(2,1)S(1)}, bf16[128,1024]{1,0:T(8,128)(2,1)}, u32[]{:S(2)}) copy-start(bf16[128,1024]{1,0:T(8,128)(2,1)} %key_ref.3) | copy-start | bytes 786436
  43.5 12.3 %copy-start.1 = (bf16[128,1024]{1,0:T(8,128)(2,1)S(1)}, bf16[128,1024]{1,0:T(8,128)(2,1)}, u32[]{:S(2)}) copy-start(bf16[128,1024]{1,0:T(8,128)(2,1)} %value_ref.3) | copy-start | bytes 786436
  56.6 6.6 %collective-permute-start.6 = (bf16[64,1024]{1,0:T(8,128)(2,1)S(1)}, bf16[64,1024]{1,0:T(8,128)(2,1)S(1)}, u32[]{:S(2)}, u32[]{:S(2)}) collective-permute-start(bf16[64,1024]{1,0:T(8,128)(2,1)S(1)} %get-tuple-element.26), channel_id=1, source_target_pairs={{0,1},{1,0},{2,3},{3,2},{4,5},{5,4},{6,7},{7,6},{8,9},{9,8},{10,11... | collective-permute-start | bytes 393224 | tf_op jit(solution)/shard_map/to_tokens/ppermute | solution.py:305

commit v5 on v4

--- a/solution.py
+++ b/solution.py
@@ -6,6 +6,7 @@
 from jax.sharding import PartitionSpec as P
 
 EPS = 1e-06
+ORDER = (2, 3, 1, 5, 6, 7, 4)
 D = 128
 ROWS = 2 * D
 SCALE = 2.0**60
@@ -75,9 +76,11 @@
 
 
 def local_compose(
-    trans_hbm, gate_hbm, key_hbm, value_hbm, wire_ref, trans_ref, gate_ref, key_ref, value_ref, sems
+    trans_hbm, gate_hbm, key_hbm, value_hbm, *refs
 ):
-    heads = range(trans_ref.shape[1])
+    *wires, trans_ref, gate_ref, key_ref, value_ref, sems = refs
+    me = lax.rem(lax.axis_index("seq"), 8)
+    heads = [me ^ d for d in range(trans_ref.shape[1])]
     rows = key_ref.shape[0] // 2
     pairs = (
         (gate_hbm, gate_ref),
@@ -93,21 +96,29 @@
     copies[2].wait()
 
     def update(c, h):
-        here = (pl.ds(c * rows, rows), pl.ds(h * D, D))
+        here = (pl.ds(c * rows, rows), pl.ds(pl.multiple_of(h * D, D), D))
         return dot(value_ref[here], key_ref[here], 0, 0)
 
     updates = [(update(0, h).astype(BF16), update(1, h)) for h in heads]
     copies[0].wait()
     copies[3].wait()
-    for h in heads:
-        first, second = updates[h]
+    for d, h in enumerate(heads):
+        first, second = updates[d]
         a1 = trans_ref[1, h]
         state = gate_ref[1, h] * dot(first, a1, 1, 1) + second
         matrix = (gate_ref[0, h] * gate_ref[1, h]) * dot(trans_ref[0, h], a1, 0, 1)
-        pack(wire_ref, (h,), jnp.concatenate([matrix, state], axis=0), eye)
-
-
-def line_total(wire_ref, total_ref):
+        pack(wires[d], (), jnp.concatenate([matrix, state], axis=0), eye)
+
+
+def sort_line(refs, sorted_ref):
+    me = lax.rem(lax.axis_index("seq"), 8)
+    for d, ref in enumerate(refs):
+        sorted_ref[me ^ d] = ref[...]
+
+
+def line_total(*refs):
+    *wires, total_ref, wire_ref = refs
+    sort_line(wires, wire_ref)
     eye = eye_mask()
     count = wire_ref.shape[0]
     runs = [
@@ -119,7 +130,9 @@
     pack(total_ref, (), runs[0], eye)
 
 
-def line_before(wire_ref, gain_in_ref, gate_in_ref, pre_ref, gain_ref, gate_ref):
+def line_before(*refs):
+    *wires, gain_in_ref, gate_in_ref, pre_ref, gain_ref, gate_ref, wire_ref = refs
+    sort_line(wires, wire_ref)
     gain_ref[...] = gain_in_ref[...]
     for h in range(gate_ref.shape[0]):
         gate_ref[pl.ds(h, 1)] = jnp.broadcast_to(gate_in_ref[0:1, h : h + 1], (1, D))
@@ -135,7 +148,8 @@
 
 def sort_ring(stride, refs, sorted_ref):
     me = lax.rem(lax.axis_index("seq") // stride, 4)
-    for d, ref in zip((0, 2, 3, 1), refs):
+    core = lax.axis_index("head")
+    for d, ref in zip((0, 2 - core, 3, 1 + core), refs):
         sorted_ref[me ^ d] = ref[...]
     return me
 
@@ -262,12 +276,13 @@
             pairs = []
             for s in range(count):
                 at = s // stride % 4
-                pairs.append((s, s + ((at ^ d) - at) * stride))
-            out.append(lax.ppermute(total, "seq", pairs))
+                for core, e in ((0, d), (1, {2: 1, 3: 3, 1: 2}[d])):
+                    pairs.append((2 * s + core, 2 * (s + ((at ^ e) - at) * stride) + core))
+            out.append(lax.ppermute(total, ("seq", "head"), pairs))
         return lax.optimization_barrier(out)
 
-    (wire,) = call(
-        local_compose, [line], transitions, gates, keys, values, specs=[ANY] * 4,
+    wires = call(
+        local_compose, [one] * heads, transitions, gates, keys, values, specs=[ANY] * 4,
         scratch=[
             pltpu.VMEM(transitions.shape, BF16),
             pltpu.SMEM(gates.shape, F32),
@@ -277,13 +292,18 @@
         ],
     )
     with jax.named_scope("to_owners"):
-        wire = lax.all_to_all(wire, "seq", 0, 0, axis_index_groups=lines, tiled=True)
-    (total,) = call(line_total, [one], wire)
+        got = [
+            lax.ppermute(wires[d], "seq", [(s, s ^ d) for s in range(count)]) for d in ORDER
+        ]
+        got = dict(zip(ORDER, lax.optimization_barrier(got)))
+        wires = [wires[0]] + [got[d] for d in range(1, heads)]
+    lined = [pltpu.VMEM(*line)]
+    (total,) = call(line_total, [one], *wires, scratch=lined)
     with jax.named_scope("along_y"):
         others = around(total, 8)
     line_pre, gain, gate = call(
         line_before, [line, ((1, D), F32), ((heads, D), F32)],
-        wire, norm_gain.reshape(1, D), gates, specs=[VMEM, PLAIN, PLAIN],
+        *wires, norm_gain.reshape(1, D), gates, specs=[VMEM] * heads + [PLAIN, PLAIN], scratch=lined,
     )
     (whole,) = call(plane_total, [one], total, *others, scratch=ring)
     with jax.named_scope("along_x"):

time: 64.1 us -> 63.4 us (0.989)
  blocking collectives: 37.1 us -> 15.4 us
  starting transfers between devices: 12.9 us -> 26.8 us
  waiting for transfers between devices: 5.85 us -> 12.8 us
    all_to_all x1 -> x0, blocking collectives: 24.8 us -> none  [shards(): lax.all_to_all(wire, 'seq', 0, 0, axis_index_groups=lines, tiled=True)]
    ppermute x6 -> x13, starting transfers between devices: 7.49 us -> 22.7 us  [the longest x7 15 us: shards(): lax.ppermute(wires[d], 'seq', [(s, s ^ d) for s in range(count)])]
    ppermute x6 -> x13, waiting for transfers between devices: 5.85 us -> 12.8 us  [the longest x7 6.88 us: shards(): lax.ppermute(wires[d], 'seq', [(s, s ^ d) for s in range(count)])]
    all_to_all x1, blocking collectives: 12.3 us -> 15.4 us  [shards(): lax.all_to_all(states, 'seq', 0, 0, axis_index_groups=lines, tiled=True)]
    ppermute x1, starting transfers between devices: 5.41 us -> 4.11 us  [shards(): other = lax.ppermute(send, 'head', [(0, 1), (1, 0)])]
  transfers between devices with their start and end apart: 7 -> 14, of which waited for: 3 -> 6; matrix products, arithmetic and copies ran while one was open for 0% -> 0% of each run, Pallas kernels for 5% -> 5%
where the time goes in v5:
time: 63.4 us; the launch traced here: 63.3 us
  starting transfers between devices  26.8 us (42%)
  blocking collectives  15.4 us (24%)
  waiting for transfers between devices  12.8 us (20%)
  Pallas kernels  7.4 us (12%)
  local copies, waits for them, and re-layouts  0.69 us (1%)
    all_to_all x1, blocking collectives, shards(): lax.all_to_all(states, 'seq', 0, 0, axis_index_groups=lines, tiled=True)  15.4 us
    ppermute x7, starting transfers between devices, shards(): lax.ppermute(wires[d], 'seq', [(s, s ^ d) for s in range(count)])  15 us
    ppermute x6, starting transfers between devices, around(): out.append(lax.ppermute(total, ('seq', 'head'), pairs))  7.7 us
    pallas_call x8, Pallas kernels, call(): pl.pallas_call(kernel, out_shape=shapes, in_specs=specs, out_specs=[ANY i...  7.4 us
    ppermute x7, waiting for transfers between devices, shards(): lax.ppermute(wires[d], 'seq', [(s, s ^ d) for s in range(count)])  6.88 us
    ppermute x6, waiting for transfers between devices, around(): out.append(lax.ppermute(total, ('seq', 'head'), pairs))  5.96 us
    ppermute x1, starting transfers between devices, shards(): other = lax.ppermute(send, 'head', [(0, 1), (1, 0)])  4.11 us
  transfers between devices with their start and end apart: 14, of which 6 were waited for; matrix products, arithmetic and copies ran while one was open for 0% of the time, Pallas kernels for 5%

profile of v5, /device:TPU:1, one launch (start us, length us, event | category | flops | bytes accessed | tf_op | source)
XLA Modules:
  0.0 63.3 jit_solution(16872527399395477009)
XLA Ops:
  0.0 1.9 %local_compose.1 = (bf16[256,128]{1,0:T(8,128)(2,1)S(1)}, bf16[256,128]{1,0:T(8,128)(2,1)S(1)}, bf16[256,128]{1,0:T(8,128)(2,1)S(1)}, bf16[256,128]{1,0:T(8,128)...) custom-call(bf16[2,8,128,128]{3,2,1,0:T(8,128)(2,1)} %trans_ref.1, ...), custom_call_target="tpu_custom_call" | custom-call | bytes 1048576 | tf_op jit(solution)/shard_map/local_compose/pallas_call | solution.py:253
  1.9 3.9 %collective-permute-start = (bf16[256,128]{1,0:T(8,128)(2,1)S(1)}, bf16[256,128]{1,0:T(8,128)(2,1)S(1)}, u32[]{:S(2)}, u32[]{:S(2)}) collective-permute-start(bf16[256,128]{1,0:T(8,128)(2,1)S(1)} %get-tuple-element.32), channel_id=1, source_target_pairs={{0,4},{2,6},{4,0},{6,2},{8,12},{10,14},{12,8},{14,10},{16,20},{18,... | collective-permute-start | bytes 196616 | tf_op jit(solution)/shard_map/to_owners/ppermute | solution.py:296
  5.8 1.4 %collective-permute-start.1 = (bf16[256,128]{1,0:T(8,128)(2,1)S(1)}, bf16[256,128]{1,0:T(8,128)(2,1)S(1)}, u32[]{:S(2)}, u32[]{:S(2)}) collective-permute-start(bf16[256,128]{1,0:T(8,128)(2,1)S(1)} %get-tuple-element.33), channel_id=1, source_target_pairs={{0,6},{2,4},{4,2},{6,0},{8,14},{10,12},{12,10},{14,8},{16,22},{18,... | collective-permute-start | bytes 196616 | tf_op jit(solution)/shard_map/to_owners/ppermute | solution.py:296
  7.2 0.2 collective-permute-start.2
  7.4 5.4 %collective-permute-start.3 = (bf16[256,128]{1,0:T(8,128)(2,1)S(1)}, bf16[256,128]{1,0:T(8,128)(2,1)S(1)}, u32[]{:S(2)}, u32[]{:S(2)}) collective-permute-start(bf16[256,128]{1,0:T(8,128)(2,1)S(1)} %get-tuple-element.35), channel_id=1, source_target_pairs={{0,10},{2,8},{4,14},{6,12},{8,2},{10,0},{12,6},{14,4},{16,26},{18,... | collective-permute-start | bytes 196616 | tf_op jit(solution)/shard_map/to_owners/ppermute | solution.py:296
  12.8 0.0 collective-permute-start.4
  12.8 0.0 collective-permute-done.refs_2_
  12.8 2.4 %collective-permute-start.5 = (bf16[256,128]{1,0:T(8,128)(2,1)S(1)}, bf16[256,128]{1,0:T(8,128)(2,1)S(1)}, u32[]{:S(2)}, u32[]{:S(2)}) collective-permute-start(bf16[256,128]{1,0:T(8,128)(2,1)S(1)} %get-tuple-element.37), channel_id=1, source_target_pairs={{0,14},{2,12},{4,10},{6,8},{8,6},{10,4},{12,2},{14,0},{16,30},{18,... | collective-permute-start | bytes 196616 | tf_op jit(solution)/shard_map/to_owners/ppermute | solution.py:296
  15.2 0.0 collective-permute-done.1.refs_3_
  15.2 1.6 %collective-permute-start.6 = (bf16[256,128]{1,0:T(8,128)(2,1)S(1)}, bf16[256,128]{1,0:T(8,128)(2,1)S(1)}, u32[]{:S(2)}, u32[]{:S(2)}) collective-permute-start(bf16[256,128]{1,0:T(8,128)(2,1)S(1)} %get-tuple-element.38), channel_id=1, source_target_pairs={{0,8},{2,10},{4,12},{6,14},{8,0},{10,2},{12,4},{14,6},{16,24},{18,... | collective-permute-start | bytes 196616 | tf_op jit(solution)/shard_map/to_owners/ppermute | solution.py:296
  16.9 0.0 collective-permute-done.2.refs_1_
  16.9 1.3 %collective-permute-done.3.refs_5_ = bf16[256,128]{1,0:T(8,128)(2,1)S(1)} collective-permute-done((bf16[256,128]{1,0:T(8,128)(2,1)S(1)}, bf16[256,128]{1,0:T(8,128)(2,1)S(1)}, u32[]{:S(2)}, u32[]{:S(2)}) %collective-permute-start.3) | collective-permute-done | bytes 65568 | tf_op jit(solution)/shard_map/to_owners/ppermute | solution.py:296
  18.2 0.9 %collective-permute-done.4.refs_6_ = bf16[256,128]{1,0:T(8,128)(2,1)S(1)} collective-permute-done((bf16[256,128]{1,0:T(8,128)(2,1)S(1)}, bf16[256,128]{1,0:T(8,128)(2,1)S(1)}, u32[]{:S(2)}, u32[]{:S(2)}) %collective-permute-start.4) | collective-permute-done | bytes 65568 | tf_op jit(solution)/shard_map/to_owners/ppermute | solution.py:296
  19.1 4.7 %collective-permute-done.5.refs_7_ = bf16[256,128]{1,0:T(8,128)(2,1)S(1)} collective-permute-done((bf16[256,128]{1,0:T(8,128)(2,1)S(1)}, bf16[256,128]{1,0:T(8,128)(2,1)S(1)}, u32[]{:S(2)}, u32[]{:S(2)}) %collective-permute-start.5) | collective-permute-done | bytes 65568 | tf_op jit(solution)/shard_map/to_owners/ppermute | solution.py:296
  23.7 0.0 collective-permute-done.6.refs_4_
  23.7 0.6 line_total.1.own_ref
  24.4 1.4 %collective-permute-start.7 = (bf16[256,128]{1,0:T(8,128)(2,1)S(1)}, bf16[256,128]{1,0:T(8,128)(2,1)S(1)}, u32[]{:S(2)}, u32[]{:S(2)}) collective-permute-start(bf16[256,128]{1,0:T(8,128)(2,1)S(1)} %line_total.1.own_ref), channel_id=1, source_target_pairs={{0,32},{1,17},{2,34},{3,19},{4,36},{5,21},{6,38},{7,23},{8,40},{9,... | collective-permute-start | bytes 196616 | tf_op jit(solution)/shard_map/along_y/ppermute | solution.py:281
  25.8 1.8 %collective-permute-start.8 = (bf16[256,128]{1,0:T(8,128)(2,1)S(1)}, bf16[256,128]{1,0:T(8,128)(2,1)S(1)}, u32[]{:S(2)}, u32[]{:S(2)}) collective-permute-start(bf16[256,128]{1,0:T(8,128)(2,1)S(1)} %line_total.1.own_ref), channel_id=1, source_target_pairs={{0,48},{1,49},{2,50},{3,51},{4,52},{5,53},{6,54},{7,55},{8,56},{9,... | collective-permute-start | bytes 196616 | tf_op jit(solution)/shard_map/along_y/ppermute | solution.py:281
  27.6 0.7 %collective-permute-start.9 = (bf16[256,128]{1,0:T(8,128)(2,1)S(1)}, bf16[256,128]{1,0:T(8,128)(2,1)S(1)}, u32[]{:S(2)}, u32[]{:S(2)}) collective-permute-start(bf16[256,128]{1,0:T(8,128)(2,1)S(1)} %line_total.1.own_ref), channel_id=1, source_target_pairs={{0,16},{1,33},{2,18},{3,35},{4,20},{5,37},{6,22},{7,39},{8,24},{9,... | collective-permute-start | bytes 196616 | tf_op jit(solution)/shard_map/along_y/ppermute | solution.py:281
  28.3 0.0 collective-permute-done.7.a_ref
  28.3 1.8 %collective-permute-done.8.b_ref = bf16[256,128]{1,0:T(8,128)(2,1)S(1)} collective-permute-done((bf16[256,128]{1,0:T(8,128)(2,1)S(1)}, bf16[256,128]{1,0:T(8,128)(2,1)S(1)}, u32[]{:S(2)}, u32[]{:S(2)}) %collective-permute-start.8) | collective-permute-done | bytes 65568 | tf_op jit(solution)/shard_map/along_y/ppermute | solution.py:281
  30.1 2.1 %collective-permute-done.9.c_ref = bf16[256,128]{1,0:T(8,128)(2,1)S(1)} collective-permute-done((bf16[256,128]{1,0:T(8,128)(2,1)S(1)}, bf16[256,128]{1,0:T(8,128)(2,1)S(1)}, u32[]{:S(2)}, u32[]{:S(2)}) %collective-permute-start.9) | collective-permute-done | bytes 65568 | tf_op jit(solution)/shard_map/along_y/ppermute | solution.py:281
  32.2 0.4 plane_total.1.own_ref
  32.6 1.3 %collective-permute-start.10 = (bf16[256,128]{1,0:T(8,128)(2,1)S(1)}, bf16[256,128]{1,0:T(8,128)(2,1)S(1)}, u32[]{:S(2)}, u32[]{:S(2)}) collective-permute-start(bf16[256,128]{1,0:T(8,128)(2,1)S(1)} %plane_total.1.own_ref), channel_id=1, source_target_pairs={{0,128},{1,65},{2,130},{3,67},{4,132},{5,69},{6,134},{7,71},{8,136... | collective-permute-start | bytes 196616 | tf_op jit(solution)/shard_map/along_x/ppermute | solution.py:281
  34.0 1.7 %collective-permute-start.11 = (bf16[256,128]{1,0:T(8,128)(2,1)S(1)}, bf16[256,128]{1,0:T(8,128)(2,1)S(1)}, u32[]{:S(2)}, u32[]{:S(2)}) collective-permute-start(bf16[256,128]{1,0:T(8,128)(2,1)S(1)} %plane_total.1.own_ref), channel_id=1, source_target_pairs={{0,192},{1,193},{2,194},{3,195},{4,196},{5,197},{6,198},{7,199},{8... | collective-permute-start | bytes 196616 | tf_op jit(solution)/shard_map/along_x/ppermute | solution.py:281
  35.7 0.7 %collective-permute-start.12 = (bf16[256,128]{1,0:T(8,128)(2,1)S(1)}, bf16[256,128]{1,0:T(8,128)(2,1)S(1)}, u32[]{:S(2)}, u32[]{:S(2)}) collective-permute-start(bf16[256,128]{1,0:T(8,128)(2,1)S(1)} %plane_total.1.own_ref), channel_id=1, source_target_pairs={{0,64},{1,129},{2,66},{3,131},{4,68},{5,133},{6,70},{7,135},{8,72}... | collective-permute-start | bytes 196616 | tf_op jit(solution)/shard_map/along_x/ppermute | solution.py:281
  36.4 1.5 %line_before.1 = (bf16[8,256,128]{2,1,0:T(8,128)(2,1)S(1)}, f32[1,128]{1,0:T(1,128)S(1)}, f32[8,128]{1,0:T(8,128)S(1)}) custom-call(bf16[256,128]{1,0:T(8,128)(2,1)S(1)} %get-tuple-element.31.refs_0_, bf16[256,128]{1,0:T(8,128)(2,1)S(1)} %collective-permute-done.2.refs_1_, bf16[256,128]{1,0:T(8,128)(2,1)S(1)} %collective-permute-done.refs_2_, ...), custom_call_target="tpu_custom_call" | custom-call | bytes 1048576 | tf_op jit(solution)/shard_map/line_before/pallas_call | solution.py:253
  37.9 0.3 plane_before.1.plane_ref
  38.3 0.0 collective-permute-done.10.a_ref
  38.3 0.0 collective-permute-done.11.b_ref
  38.3 2.0 %collective-permute-done.12.c_ref = bf16[256,128]{1,0:T(8,128)(2,1)S(1)} collective-permute-done((bf16[256,128]{1,0:T(8,128)(2,1)S(1)}, bf16[256,128]{1,0:T(8,128)(2,1)S(1)}, u32[]{:S(2)}, u32[]{:S(2)}) %collective-permute-start.12) | collective-permute-done | bytes 65568 | tf_op jit(solution)/shard_map/along_x/ppermute | solution.py:281
  40.3 0.0 copy-start.2
  40.3 0.0 copy-start.3
  40.3 0.6 enter_states.1
  41.0 0.0 copy-start
  41.0 0.0 copy-start.1
  41.0 15.4 %all_to_all.5.state_ref = bf16[8,128,128]{2,1,0:T(8,128)(2,1)S(1)} all-to-all(bf16[8,128,128]{2,1,0:T(8,128)(2,1)S(1)} %enter_states.1), channel_id=1, replica_groups={{0,2,4,6,8,10,12,14},{16,18,20,22,24,26,28,30},{32,34,36,38,40,42,44,46..., dimensions={0} | all-to-all | bytes 524288 | tf_op jit(solution)/shard_map/from_owners/all_to_all | solution.py:316
  56.4 0.0 copy-done.2
  56.4 0.0 copy-done.3
  56.4 0.0 copy-done
  56.4 0.0 copy-done.1
  56.5 0.8 %sent_outputs.1 = (bf16[64,1024]{1,0:T(8,128)(2,1)S(1)}, bf16[8,128,128]{2,1,0:T(8,128)(2,1)S(1)}) custom-call(bf16[128,1024]{1,0:T(8,128)(2,1)S(1)} %copy-done.3, bf16[128,1024]{1,0:T(8,128)(2,1)S(1)} %copy-done, bf16[128,1024]{1,0:T(8,128)(2,1)S(1)} %copy-done.1, bf16[2,8,128,128]{3,2,1,0:T(8,128)(2,1)S(1)} %copy-done.2, ...), custom_call_target="tpu_custom_call" | custom-call | bytes 1048576 | tf_op jit(solution)/shard_map/sent_outputs/pallas_call | solution.py:253
  57.2 4.1 %collective-permute-start.13 = (bf16[64,1024]{1,0:T(8,128)(2,1)S(1)}, bf16[64,1024]{1,0:T(8,128)(2,1)S(1)}, u32[]{:S(2)}, u32[]{:S(2)}) collective-permute-start(bf16[64,1024]{1,0:T(8,128)(2,1)S(1)} %get-tuple-element.56), channel_id=1, source_target_pairs={{0,1},{1,0},{2,3},{3,2},{4,5},{5,4},{6,7},{7,6},{8,9},{9,8},{10,11... | collective-permute-start | bytes 393224 | tf_op jit(solution)/shard_map/to_tokens/ppermute | solution.py:325
  61.4 1.2 %kept_outputs.1 = bf16[64,2048]{1,0:T(8,128)(2,1)} custom-call(bf16[128,1024]{1,0:T(8,128)(2,1)S(1)} %copy-done.3, bf16[128,1024]{1,0:T(8,128)(2,1)S(1)} %copy-done, bf16[128,1024]{1,0:T(8,128)(2,1)S(1)} %copy-done.1, bf16[8,128,128]{2,1,0:T(8,128)(2,1)S(1)} %get-tuple-element.55.state_ref, f32[1,128]{1,0:T(1,128)S(1)} %get-tuple-element.54.gain_ref), custom_call_target="tpu_custom_call" | custom-call | bytes 1048576 | tf_op jit(solution)/shard_map/kept_outputs/pallas_call | solution.py:253
  62.6 0.0 collective-permute-done.13
  62.6 0.7 %constant_dynamic-update-slice_fusion = bf16[64,2048]{1,0:T(8,128)(2,1)} fusion(bf16[64,2048]{1,0:T(8,128)(2,1)} %kept_outputs.1, bf16[64,1024]{1,0:T(8,128)(2,1)S(1)} %collective-permute-done.13, s32[]{:T(128)S(6)} %select_n.3), kind=kLoop, calls=%fused_computation | loop fusion | bytes 262148 | tf_op jit(solution)/shard_map/dynamic_update_slice | solution.py:332
Async XLA Ops:
  1.9 10.9 %collective-permute-start = (bf16[256,128]{1,0:T(8,128)(2,1)S(1)}, bf16[256,128]{1,0:T(8,128)(2,1)S(1)}, u32[]{:S(2)}, u32[]{:S(2)}) collective-permute-start(bf16[256,128]{1,0:T(8,128)(2,1)S(1)} %get-tuple-element.32), channel_id=1, source_target_pairs={{0,4},{2,6},{4,0},{6,2},{8,12},{10,14},{12,8},{14,10},{16,20},{18,... | collective-permute-start | bytes 196616 | tf_op jit(solution)/shard_map/to_owners/ppermute | solution.py:296
  5.8 9.4 %collective-permute-start.1 = (bf16[256,128]{1,0:T(8,128)(2,1)S(1)}, bf16[256,128]{1,0:T(8,128)(2,1)S(1)}, u32[]{:S(2)}, u32[]{:S(2)}) collective-permute-start(bf16[256,128]{1,0:T(8,128)(2,1)S(1)} %get-tuple-element.33), channel_id=1, source_target_pairs={{0,6},{2,4},{4,2},{6,0},{8,14},{10,12},{12,10},{14,8},{16,22},{18,... | collective-permute-start | bytes 196616 | tf_op jit(solution)/shard_map/to_owners/ppermute | solution.py:296
  7.2 9.6 %collective-permute-start.2 = (bf16[256,128]{1,0:T(8,128)(2,1)S(1)}, bf16[256,128]{1,0:T(8,128)(2,1)S(1)}, u32[]{:S(2)}, u32[]{:S(2)}) collective-permute-start(bf16[256,128]{1,0:T(8,128)(2,1)S(1)} %get-tuple-element.34), channel_id=1, source_target_pairs={{0,2},{2,0},{4,6},{6,4},{8,10},{10,8},{12,14},{14,12},{16,18},{18,... | collective-permute-start | bytes 196616 | tf_op jit(solution)/shard_map/to_owners/ppermute | solution.py:296
  7.4 10.8 %collective-permute-start.3 = (bf16[256,128]{1,0:T(8,128)(2,1)S(1)}, bf16[256,128]{1,0:T(8,128)(2,1)S(1)}, u32[]{:S(2)}, u32[]{:S(2)}) collective-permute-start(bf16[256,128]{1,0:T(8,128)(2,1)S(1)} %get-tuple-element.35), channel_id=1, source_target_pairs={{0,10},{2,8},{4,14},{6,12},{8,2},{10,0},{12,6},{14,4},{16,26},{18,... | collective-permute-start | bytes 196616 | tf_op jit(solution)/shard_map/to_owners/ppermute | solution.py:296
  12.8 6.2 %collective-permute-start.4 = (bf16[256,128]{1,0:T(8,128)(2,1)S(1)}, bf16[256,128]{1,0:T(8,128)(2,1)S(1)}, u32[]{:S(2)}, u32[]{:S(2)}) collective-permute-start(bf16[256,128]{1,0:T(8,128)(2,1)S(1)} %get-tuple-element.36), channel_id=1, source_target_pairs={{0,12},{2,14},{4,8},{6,10},{8,4},{10,6},{12,0},{14,2},{16,28},{18,... | collective-permute-start | bytes 196616 | tf_op jit(solution)/shard_map/to_owners/ppermute | solution.py:296
  12.8 10.9 %collective-permute-start.5 = (bf16[256,128]{1,0:T(8,128)(2,1)S(1)}, bf16[256,128]{1,0:T(8,128)(2,1)S(1)}, u32[]{:S(2)}, u32[]{:S(2)}) collective-permute-start(bf16[256,128]{1,0:T(8,128)(2,1)S(1)} %get-tuple-element.37), channel_id=1, source_target_pairs={{0,14},{2,12},{4,10},{6,8},{8,6},{10,4},{12,2},{14,0},{16,30},{18,... | collective-permute-start | bytes 196616 | tf_op jit(solution)/shard_map/to_owners/ppermute | solution.py:296
  15.2 8.5 %collective-permute-start.6 = (bf16[256,128]{1,0:T(8,128)(2,1)S(1)}, bf16[256,128]{1,0:T(8,128)(2,1)S(1)}, u32[]{:S(2)}, u32[]{:S(2)}) collective-permute-start(bf16[256,128]{1,0:T(8,128)(2,1)S(1)} %get-tuple-element.38), channel_id=1, source_target_pairs={{0,8},{2,10},{4,12},{6,14},{8,0},{10,2},{12,4},{14,6},{16,24},{18,... | collective-permute-start | bytes 196616 | tf_op jit(solution)/shard_map/to_owners/ppermute | solution.py:296
  24.4 4.0 %collective-permute-start.7 = (bf16[256,128]{1,0:T(8,128)(2,1)S(1)}, bf16[256,128]{1,0:T(8,128)(2,1)S(1)}, u32[]{:S(2)}, u32[]{:S(2)}) collective-permute-start(bf16[256,128]{1,0:T(8,128)(2,1)S(1)} %line_total.1.own_ref), channel_id=1, source_target_pairs={{0,32},{1,17},{2,34},{3,19},{4,36},{5,21},{6,38},{7,23},{8,40},{9,... | collective-permute-start | bytes 196616 | tf_op jit(solution)/shard_map/along_y/ppermute | solution.py:281
  25.8 4.3 %collective-permute-start.8 = (bf16[256,128]{1,0:T(8,128)(2,1)S(1)}, bf16[256,128]{1,0:T(8,128)(2,1)S(1)}, u32[]{:S(2)}, u32[]{:S(2)}) collective-permute-start(bf16[256,128]{1,0:T(8,128)(2,1)S(1)} %line_total.1.own_ref), channel_id=1, source_target_pairs={{0,48},{1,49},{2,50},{3,51},{4,52},{5,53},{6,54},{7,55},{8,56},{9,... | collective-permute-start | bytes 196616 | tf_op jit(solution)/shard_map/along_y/ppermute | solution.py:281
  27.6 4.6 %collective-permute-start.9 = (bf16[256,128]{1,0:T(8,128)(2,1)S(1)}, bf16[256,128]{1,0:T(8,128)(2,1)S(1)}, u32[]{:S(2)}, u32[]{:S(2)}) collective-permute-start(bf16[256,128]{1,0:T(8,128)(2,1)S(1)} %line_total.1.own_ref), channel_id=1, source_target_pairs={{0,16},{1,33},{2,18},{3,35},{4,20},{5,37},{6,22},{7,39},{8,24},{9,... | collective-permute-start | bytes 196616 | tf_op jit(solution)/shard_map/along_y/ppermute | solution.py:281
  32.6 5.6 %collective-permute-start.10 = (bf16[256,128]{1,0:T(8,128)(2,1)S(1)}, bf16[256,128]{1,0:T(8,128)(2,1)S(1)}, u32[]{:S(2)}, u32[]{:S(2)}) collective-permute-start(bf16[256,128]{1,0:T(8,128)(2,1)S(1)} %plane_total.1.own_ref), channel_id=1, source_target_pairs={{0,128},{1,65},{2,130},{3,67},{4,132},{5,69},{6,134},{7,71},{8,136... | collective-permute-start | bytes 196616 | tf_op jit(solution)/shard_map/along_x/ppermute | solution.py:281
  34.0 4.3 %collective-permute-start.11 = (bf16[256,128]{1,0:T(8,128)(2,1)S(1)}, bf16[256,128]{1,0:T(8,128)(2,1)S(1)}, u32[]{:S(2)}, u32[]{:S(2)}) collective-permute-start(bf16[256,128]{1,0:T(8,128)(2,1)S(1)} %plane_total.1.own_ref), channel_id=1, source_target_pairs={{0,192},{1,193},{2,194},{3,195},{4,196},{5,197},{6,198},{7,199},{8... | collective-permute-start | bytes 196616 | tf_op jit(solution)/shard_map/along_x/ppermute | solution.py:281
  35.7 4.6 %collective-permute-start.12 = (bf16[256,128]{1,0:T(8,128)(2,1)S(1)}, bf16[256,128]{1,0:T(8,128)(2,1)S(1)}, u32[]{:S(2)}, u32[]{:S(2)}) collective-permute-start(bf16[256,128]{1,0:T(8,128)(2,1)S(1)} %plane_total.1.own_ref), channel_id=1, source_target_pairs={{0,64},{1,129},{2,66},{3,131},{4,68},{5,133},{6,70},{7,135},{8,72}... | collective-permute-start | bytes 196616 | tf_op jit(solution)/shard_map/along_x/ppermute | solution.py:281
  40.3 16.1 %copy-start.2 = (bf16[2,8,128,128]{3,2,1,0:T(8,128)(2,1)S(1)}, bf16[2,8,128,128]{3,2,1,0:T(8,128)(2,1)}, u32[]{:S(2)}) copy-start(bf16[2,8,128,128]{3,2,1,0:T(8,128)(2,1)} %trans_ref.1) | copy-start | bytes 1572868
  40.3 16.1 %copy-start.3 = (bf16[128,1024]{1,0:T(8,128)(2,1)S(1)}, bf16[128,1024]{1,0:T(8,128)(2,1)}, u32[]{:S(2)}) copy-start(bf16[128,1024]{1,0:T(8,128)(2,1)} %query_ref.3) | copy-start | bytes 786436
  41.0 15.5 %copy-start = (bf16[128,1024]{1,0:T(8,128)(2,1)S(1)}, bf16[128,1024]{1,0:T(8,128)(2,1)}, u32[]{:S(2)}) copy-start(bf16[128,1024]{1,0:T(8,128)(2,1)} %key_ref.3) | copy-start | bytes 786436
  41.0 15.5 %copy-start.1 = (bf16[128,1024]{1,0:T(8,128)(2,1)S(1)}, bf16[128,1024]{1,0:T(8,128)(2,1)}, u32[]{:S(2)}) copy-start(bf16[128,1024]{1,0:T(8,128)(2,1)} %value_ref.3) | copy-start | bytes 786436
  57.2 5.3 %collective-permute-start.13 = (bf16[64,1024]{1,0:T(8,128)(2,1)S(1)}, bf16[64,1024]{1,0:T(8,128)(2,1)S(1)}, u32[]{:S(2)}, u32[]{:S(2)}) collective-permute-start(bf16[64,1024]{1,0:T(8,128)(2,1)S(1)} %get-tuple-element.56), channel_id=1, source_target_pairs={{0,1},{1,0},{2,3},{3,2},{4,5},{5,4},{6,7},{7,6},{8,9},{9,8},{10,11... | collective-permute-start | bytes 393224 | tf_op jit(solution)/shard_map/to_tokens/ppermute | solution.py:325

commit v6 on v5

--- a/solution.py
+++ b/solution.py
@@ -305,6 +305,7 @@
         line_before, [line, ((1, D), F32), ((heads, D), F32)],
         *wires, norm_gain.reshape(1, D), gates, specs=[VMEM] * heads + [PLAIN, PLAIN], scratch=lined,
     )
+    others, line_pre = lax.optimization_barrier((others, line_pre))
     (whole,) = call(plane_total, [one], total, *others, scratch=ring)
     with jax.named_scope("along_x"):
         planes = around(whole, 32)

time: 63.4 us -> 63.4 us (level)
  transfers between devices with their start and end apart: 14 -> 14, of which waited for: 6 -> 7; matrix products, arithmetic and copies ran while one was open for 0% -> 0% of each run, Pallas kernels for 5% -> 5%
where the time goes in v6:
time: 63.4 us; the launch traced here: 63.3 us
  starting transfers between devices  26.8 us (42%)
  blocking collectives  15.4 us (24%)
  waiting for transfers between devices  12.8 us (20%)
  Pallas kernels  7.4 us (12%)
  local copies, waits for them, and re-layouts  0.69 us (1%)
    all_to_all x1, blocking collectives, shards(): lax.all_to_all(states, 'seq', 0, 0, axis_index_groups=lines, tiled=True)  15.4 us
    ppermute x7, starting transfers between devices, shards(): lax.ppermute(wires[d], 'seq', [(s, s ^ d) for s in range(count)])  15 us
    ppermute x6, starting transfers between devices, around(): out.append(lax.ppermute(total, ('seq', 'head'), pairs))  7.7 us
    pallas_call x8, Pallas kernels, call(): pl.pallas_call(kernel, out_shape=shapes, in_specs=specs, out_specs=[ANY i...  7.4 us
    ppermute x7, waiting for transfers between devices, shards(): lax.ppermute(wires[d], 'seq', [(s, s ^ d) for s in range(count)])  6.88 us
    ppermute x6, waiting for transfers between devices, around(): out.append(lax.ppermute(total, ('seq', 'head'), pairs))  5.96 us
    ppermute x1, starting transfers between devices, shards(): other = lax.ppermute(send, 'head', [(0, 1), (1, 0)])  4.11 us
  transfers between devices with their start and end apart: 14, of which 7 were waited for; matrix products, arithmetic and copies ran while one was open for 0% of the time, Pallas kernels for 5%

profile of v6, /device:TPU:1, one launch (start us, length us, event | category | flops | bytes accessed | tf_op | source)
XLA Modules:
  0.0 63.3 jit_solution(5050849180590219269)
XLA Ops:
  0.0 1.9 %local_compose.1 = (bf16[256,128]{1,0:T(8,128)(2,1)S(1)}, bf16[256,128]{1,0:T(8,128)(2,1)S(1)}, bf16[256,128]{1,0:T(8,128)(2,1)S(1)}, bf16[256,128]{1,0:T(8,128)...) custom-call(bf16[2,8,128,128]{3,2,1,0:T(8,128)(2,1)} %trans_ref.1, ...), custom_call_target="tpu_custom_call" | custom-call | bytes 1048576 | tf_op jit(solution)/shard_map/local_compose/pallas_call | solution.py:253
  1.9 3.9 %collective-permute-start = (bf16[256,128]{1,0:T(8,128)(2,1)S(1)}, bf16[256,128]{1,0:T(8,128)(2,1)S(1)}, u32[]{:S(2)}, u32[]{:S(2)}) collective-permute-start(bf16[256,128]{1,0:T(8,128)(2,1)S(1)} %get-tuple-element.36), channel_id=1, source_target_pairs={{0,4},{2,6},{4,0},{6,2},{8,12},{10,14},{12,8},{14,10},{16,20},{18,... | collective-permute-start | bytes 196616 | tf_op jit(solution)/shard_map/to_owners/ppermute | solution.py:296
  5.8 1.4 %collective-permute-start.1 = (bf16[256,128]{1,0:T(8,128)(2,1)S(1)}, bf16[256,128]{1,0:T(8,128)(2,1)S(1)}, u32[]{:S(2)}, u32[]{:S(2)}) collective-permute-start(bf16[256,128]{1,0:T(8,128)(2,1)S(1)} %get-tuple-element.37), channel_id=1, source_target_pairs={{0,6},{2,4},{4,2},{6,0},{8,14},{10,12},{12,10},{14,8},{16,22},{18,... | collective-permute-start | bytes 196616 | tf_op jit(solution)/shard_map/to_owners/ppermute | solution.py:296
  7.2 0.2 collective-permute-start.2
  7.4 5.4 %collective-permute-start.3 = (bf16[256,128]{1,0:T(8,128)(2,1)S(1)}, bf16[256,128]{1,0:T(8,128)(2,1)S(1)}, u32[]{:S(2)}, u32[]{:S(2)}) collective-permute-start(bf16[256,128]{1,0:T(8,128)(2,1)S(1)} %get-tuple-element.39), channel_id=1, source_target_pairs={{0,10},{2,8},{4,14},{6,12},{8,2},{10,0},{12,6},{14,4},{16,26},{18,... | collective-permute-start | bytes 196616 | tf_op jit(solution)/shard_map/to_owners/ppermute | solution.py:296
  12.8 0.0 collective-permute-start.4
  12.8 0.0 collective-permute-done.refs_2_
  12.8 2.4 %collective-permute-start.5 = (bf16[256,128]{1,0:T(8,128)(2,1)S(1)}, bf16[256,128]{1,0:T(8,128)(2,1)S(1)}, u32[]{:S(2)}, u32[]{:S(2)}) collective-permute-start(bf16[256,128]{1,0:T(8,128)(2,1)S(1)} %get-tuple-element.41), channel_id=1, source_target_pairs={{0,14},{2,12},{4,10},{6,8},{8,6},{10,4},{12,2},{14,0},{16,30},{18,... | collective-permute-start | bytes 196616 | tf_op jit(solution)/shard_map/to_owners/ppermute | solution.py:296
  15.2 0.0 collective-permute-done.1.refs_3_
  15.2 1.6 %collective-permute-start.6 = (bf16[256,128]{1,0:T(8,128)(2,1)S(1)}, bf16[256,128]{1,0:T(8,128)(2,1)S(1)}, u32[]{:S(2)}, u32[]{:S(2)}) collective-permute-start(bf16[256,128]{1,0:T(8,128)(2,1)S(1)} %get-tuple-element.42), channel_id=1, source_target_pairs={{0,8},{2,10},{4,12},{6,14},{8,0},{10,2},{12,4},{14,6},{16,24},{18,... | collective-permute-start | bytes 196616 | tf_op jit(solution)/shard_map/to_owners/ppermute | solution.py:296
  16.9 0.0 collective-permute-done.2.refs_1_
  16.9 1.3 %collective-permute-done.3.refs_5_ = bf16[256,128]{1,0:T(8,128)(2,1)S(1)} collective-permute-done((bf16[256,128]{1,0:T(8,128)(2,1)S(1)}, bf16[256,128]{1,0:T(8,128)(2,1)S(1)}, u32[]{:S(2)}, u32[]{:S(2)}) %collective-permute-start.3) | collective-permute-done | bytes 65568 | tf_op jit(solution)/shard_map/to_owners/ppermute | solution.py:296
  18.2 0.9 %collective-permute-done.4.refs_6_ = bf16[256,128]{1,0:T(8,128)(2,1)S(1)} collective-permute-done((bf16[256,128]{1,0:T(8,128)(2,1)S(1)}, bf16[256,128]{1,0:T(8,128)(2,1)S(1)}, u32[]{:S(2)}, u32[]{:S(2)}) %collective-permute-start.4) | collective-permute-done | bytes 65568 | tf_op jit(solution)/shard_map/to_owners/ppermute | solution.py:296
  19.1 4.7 %collective-permute-done.5.refs_7_ = bf16[256,128]{1,0:T(8,128)(2,1)S(1)} collective-permute-done((bf16[256,128]{1,0:T(8,128)(2,1)S(1)}, bf16[256,128]{1,0:T(8,128)(2,1)S(1)}, u32[]{:S(2)}, u32[]{:S(2)}) %collective-permute-start.5) | collective-permute-done | bytes 65568 | tf_op jit(solution)/shard_map/to_owners/ppermute | solution.py:296
  23.7 0.0 collective-permute-done.6.refs_4_
  23.7 0.6 line_total.1.own_ref
  24.4 1.4 %collective-permute-start.7 = (bf16[256,128]{1,0:T(8,128)(2,1)S(1)}, bf16[256,128]{1,0:T(8,128)(2,1)S(1)}, u32[]{:S(2)}, u32[]{:S(2)}) collective-permute-start(bf16[256,128]{1,0:T(8,128)(2,1)S(1)} %line_total.1.own_ref), channel_id=1, source_target_pairs={{0,32},{1,17},{2,34},{3,19},{4,36},{5,21},{6,38},{7,23},{8,40},{9,... | collective-permute-start | bytes 196616 | tf_op jit(solution)/shard_map/along_y/ppermute | solution.py:281
  25.8 1.8 %collective-permute-start.8 = (bf16[256,128]{1,0:T(8,128)(2,1)S(1)}, bf16[256,128]{1,0:T(8,128)(2,1)S(1)}, u32[]{:S(2)}, u32[]{:S(2)}) collective-permute-start(bf16[256,128]{1,0:T(8,128)(2,1)S(1)} %line_total.1.own_ref), channel_id=1, source_target_pairs={{0,48},{1,49},{2,50},{3,51},{4,52},{5,53},{6,54},{7,55},{8,56},{9,... | collective-permute-start | bytes 196616 | tf_op jit(solution)/shard_map/along_y/ppermute | solution.py:281
  27.6 0.7 %collective-permute-start.9 = (bf16[256,128]{1,0:T(8,128)(2,1)S(1)}, bf16[256,128]{1,0:T(8,128)(2,1)S(1)}, u32[]{:S(2)}, u32[]{:S(2)}) collective-permute-start(bf16[256,128]{1,0:T(8,128)(2,1)S(1)} %line_total.1.own_ref), channel_id=1, source_target_pairs={{0,16},{1,33},{2,18},{3,35},{4,20},{5,37},{6,22},{7,39},{8,24},{9,... | collective-permute-start | bytes 196616 | tf_op jit(solution)/shard_map/along_y/ppermute | solution.py:281
  28.3 1.5 %line_before.1 = (bf16[8,256,128]{2,1,0:T(8,128)(2,1)S(1)}, f32[1,128]{1,0:T(1,128)S(1)}, f32[8,128]{1,0:T(8,128)S(1)}) custom-call(bf16[256,128]{1,0:T(8,128)(2,1)S(1)} %get-tuple-element.35.refs_0_, bf16[256,128]{1,0:T(8,128)(2,1)S(1)} %collective-permute-done.2.refs_1_, bf16[256,128]{1,0:T(8,128)(2,1)S(1)} %collective-permute-done.refs_2_, ...), custom_call_target="tpu_custom_call" | custom-call | bytes 1048576 | tf_op jit(solution)/shard_map/line_before/pallas_call | solution.py:253
  29.9 0.0 collective-permute-done.7.a_ref
  29.9 0.2 collective-permute-done.8.b_ref
  30.1 2.1 %collective-permute-done.9.c_ref = bf16[256,128]{1,0:T(8,128)(2,1)S(1)} collective-permute-done((bf16[256,128]{1,0:T(8,128)(2,1)S(1)}, bf16[256,128]{1,0:T(8,128)(2,1)S(1)}, u32[]{:S(2)}, u32[]{:S(2)}) %collective-permute-start.9) | collective-permute-done | bytes 65568 | tf_op jit(solution)/shard_map/along_y/ppermute | solution.py:281
  32.2 0.4 plane_total.1.own_ref
  32.6 1.3 %collective-permute-start.10 = (bf16[256,128]{1,0:T(8,128)(2,1)S(1)}, bf16[256,128]{1,0:T(8,128)(2,1)S(1)}, u32[]{:S(2)}, u32[]{:S(2)}) collective-permute-start(bf16[256,128]{1,0:T(8,128)(2,1)S(1)} %plane_total.1.own_ref), channel_id=1, source_target_pairs={{0,128},{1,65},{2,130},{3,67},{4,132},{5,69},{6,134},{7,71},{8,136... | collective-permute-start | bytes 196616 | tf_op jit(solution)/shard_map/along_x/ppermute | solution.py:281
  34.0 1.7 %collective-permute-start.11 = (bf16[256,128]{1,0:T(8,128)(2,1)S(1)}, bf16[256,128]{1,0:T(8,128)(2,1)S(1)}, u32[]{:S(2)}, u32[]{:S(2)}) collective-permute-start(bf16[256,128]{1,0:T(8,128)(2,1)S(1)} %plane_total.1.own_ref), channel_id=1, source_target_pairs={{0,192},{1,193},{2,194},{3,195},{4,196},{5,197},{6,198},{7,199},{8... | collective-permute-start | bytes 196616 | tf_op jit(solution)/shard_map/along_x/ppermute | solution.py:281
  35.7 0.7 %collective-permute-start.12 = (bf16[256,128]{1,0:T(8,128)(2,1)S(1)}, bf16[256,128]{1,0:T(8,128)(2,1)S(1)}, u32[]{:S(2)}, u32[]{:S(2)}) collective-permute-start(bf16[256,128]{1,0:T(8,128)(2,1)S(1)} %plane_total.1.own_ref), channel_id=1, source_target_pairs={{0,64},{1,129},{2,66},{3,131},{4,68},{5,133},{6,70},{7,135},{8,72}... | collective-permute-start | bytes 196616 | tf_op jit(solution)/shard_map/along_x/ppermute | solution.py:281
  36.4 0.3 plane_before.1.plane_ref
  36.7 0.0 collective-permute-done.10.a_ref
  36.7 1.6 %collective-permute-done.11.b_ref = bf16[256,128]{1,0:T(8,128)(2,1)S(1)} collective-permute-done((bf16[256,128]{1,0:T(8,128)(2,1)S(1)}, bf16[256,128]{1,0:T(8,128)(2,1)S(1)}, u32[]{:S(2)}, u32[]{:S(2)}) %collective-permute-start.11) | collective-permute-done | bytes 65568 | tf_op jit(solution)/shard_map/along_x/ppermute | solution.py:281
  38.3 2.0 %collective-permute-done.12.c_ref = bf16[256,128]{1,0:T(8,128)(2,1)S(1)} collective-permute-done((bf16[256,128]{1,0:T(8,128)(2,1)S(1)}, bf16[256,128]{1,0:T(8,128)(2,1)S(1)}, u32[]{:S(2)}, u32[]{:S(2)}) %collective-permute-start.12) | collective-permute-done | bytes 65568 | tf_op jit(solution)/shard_map/along_x/ppermute | solution.py:281
  40.3 0.0 copy-start.2
  40.3 0.0 copy-start.3
  40.3 0.6 enter_states.1
  41.0 0.0 copy-start
  41.0 0.0 copy-start.1
  41.0 15.4 %all_to_all.5.state_ref = bf16[8,128,128]{2,1,0:T(8,128)(2,1)S(1)} all-to-all(bf16[8,128,128]{2,1,0:T(8,128)(2,1)S(1)} %enter_states.1), channel_id=1, replica_groups={{0,2,4,6,8,10,12,14},{16,18,20,22,24,26,28,30},{32,34,36,38,40,42,44,46..., dimensions={0} | all-to-all | bytes 524288 | tf_op jit(solution)/shard_map/from_owners/all_to_all | solution.py:317
  56.4 0.0 copy-done.2
  56.4 0.0 copy-done.3
  56.4 0.0 copy-done
  56.4 0.0 copy-done.1
  56.5 0.8 %sent_outputs.1 = (bf16[64,1024]{1,0:T(8,128)(2,1)S(1)}, bf16[8,128,128]{2,1,0:T(8,128)(2,1)S(1)}) custom-call(bf16[128,1024]{1,0:T(8,128)(2,1)S(1)} %copy-done.3, bf16[128,1024]{1,0:T(8,128)(2,1)S(1)} %copy-done, bf16[128,1024]{1,0:T(8,128)(2,1)S(1)} %copy-done.1, bf16[2,8,128,128]{3,2,1,0:T(8,128)(2,1)S(1)} %copy-done.2, ...), custom_call_target="tpu_custom_call" | custom-call | bytes 1048576 | tf_op jit(solution)/shard_map/sent_outputs/pallas_call | solution.py:253
  57.2 4.1 %collective-permute-start.13 = (bf16[64,1024]{1,0:T(8,128)(2,1)S(1)}, bf16[64,1024]{1,0:T(8,128)(2,1)S(1)}, u32[]{:S(2)}, u32[]{:S(2)}) collective-permute-start(bf16[64,1024]{1,0:T(8,128)(2,1)S(1)} %get-tuple-element.64), channel_id=1, source_target_pairs={{0,1},{1,0},{2,3},{3,2},{4,5},{5,4},{6,7},{7,6},{8,9},{9,8},{10,11... | collective-permute-start | bytes 393224 | tf_op jit(solution)/shard_map/to_tokens/ppermute | solution.py:326
  61.4 1.2 %kept_outputs.1 = bf16[64,2048]{1,0:T(8,128)(2,1)} custom-call(bf16[128,1024]{1,0:T(8,128)(2,1)S(1)} %copy-done.3, bf16[128,1024]{1,0:T(8,128)(2,1)S(1)} %copy-done, bf16[128,1024]{1,0:T(8,128)(2,1)S(1)} %copy-done.1, bf16[8,128,128]{2,1,0:T(8,128)(2,1)S(1)} %get-tuple-element.63.state_ref, f32[1,128]{1,0:T(1,128)S(1)} %get-tuple-element.62.gain_ref), custom_call_target="tpu_custom_call" | custom-call | bytes 1048576 | tf_op jit(solution)/shard_map/kept_outputs/pallas_call | solution.py:253
  62.6 0.0 collective-permute-done.13
  62.6 0.7 %constant_dynamic-update-slice_fusion = bf16[64,2048]{1,0:T(8,128)(2,1)} fusion(bf16[64,2048]{1,0:T(8,128)(2,1)} %kept_outputs.1, bf16[64,1024]{1,0:T(8,128)(2,1)S(1)} %collective-permute-done.13, s32[]{:T(128)S(6)} %select_n.3), kind=kLoop, calls=%fused_computation | loop fusion | bytes 262148 | tf_op jit(solution)/shard_map/dynamic_update_slice | solution.py:333
Async XLA Ops:
  1.9 10.9 %collective-permute-start = (bf16[256,128]{1,0:T(8,128)(2,1)S(1)}, bf16[256,128]{1,0:T(8,128)(2,1)S(1)}, u32[]{:S(2)}, u32[]{:S(2)}) collective-permute-start(bf16[256,128]{1,0:T(8,128)(2,1)S(1)} %get-tuple-element.36), channel_id=1, source_target_pairs={{0,4},{2,6},{4,0},{6,2},{8,12},{10,14},{12,8},{14,10},{16,20},{18,... | collective-permute-start | bytes 196616 | tf_op jit(solution)/shard_map/to_owners/ppermute | solution.py:296
  5.8 9.4 %collective-permute-start.1 = (bf16[256,128]{1,0:T(8,128)(2,1)S(1)}, bf16[256,128]{1,0:T(8,128)(2,1)S(1)}, u32[]{:S(2)}, u32[]{:S(2)}) collective-permute-start(bf16[256,128]{1,0:T(8,128)(2,1)S(1)} %get-tuple-element.37), channel_id=1, source_target_pairs={{0,6},{2,4},{4,2},{6,0},{8,14},{10,12},{12,10},{14,8},{16,22},{18,... | collective-permute-start | bytes 196616 | tf_op jit(solution)/shard_map/to_owners/ppermute | solution.py:296
  7.2 9.6 %collective-permute-start.2 = (bf16[256,128]{1,0:T(8,128)(2,1)S(1)}, bf16[256,128]{1,0:T(8,128)(2,1)S(1)}, u32[]{:S(2)}, u32[]{:S(2)}) collective-permute-start(bf16[256,128]{1,0:T(8,128)(2,1)S(1)} %get-tuple-element.38), channel_id=1, source_target_pairs={{0,2},{2,0},{4,6},{6,4},{8,10},{10,8},{12,14},{14,12},{16,18},{18,... | collective-permute-start | bytes 196616 | tf_op jit(solution)/shard_map/to_owners/ppermute | solution.py:296
  7.4 10.8 %collective-permute-start.3 = (bf16[256,128]{1,0:T(8,128)(2,1)S(1)}, bf16[256,128]{1,0:T(8,128)(2,1)S(1)}, u32[]{:S(2)}, u32[]{:S(2)}) collective-permute-start(bf16[256,128]{1,0:T(8,128)(2,1)S(1)} %get-tuple-element.39), channel_id=1, source_target_pairs={{0,10},{2,8},{4,14},{6,12},{8,2},{10,0},{12,6},{14,4},{16,26},{18,... | collective-permute-start | bytes 196616 | tf_op jit(solution)/shard_map/to_owners/ppermute | solution.py:296
  12.8 6.2 %collective-permute-start.4 = (bf16[256,128]{1,0:T(8,128)(2,1)S(1)}, bf16[256,128]{1,0:T(8,128)(2,1)S(1)}, u32[]{:S(2)}, u32[]{:S(2)}) collective-permute-start(bf16[256,128]{1,0:T(8,128)(2,1)S(1)} %get-tuple-element.40), channel_id=1, source_target_pairs={{0,12},{2,14},{4,8},{6,10},{8,4},{10,6},{12,0},{14,2},{16,28},{18,... | collective-permute-start | bytes 196616 | tf_op jit(solution)/shard_map/to_owners/ppermute | solution.py:296
  12.8 10.9 %collective-permute-start.5 = (bf16[256,128]{1,0:T(8,128)(2,1)S(1)}, bf16[256,128]{1,0:T(8,128)(2,1)S(1)}, u32[]{:S(2)}, u32[]{:S(2)}) collective-permute-start(bf16[256,128]{1,0:T(8,128)(2,1)S(1)} %get-tuple-element.41), channel_id=1, source_target_pairs={{0,14},{2,12},{4,10},{6,8},{8,6},{10,4},{12,2},{14,0},{16,30},{18,... | collective-permute-start | bytes 196616 | tf_op jit(solution)/shard_map/to_owners/ppermute | solution.py:296
  15.2 8.5 %collective-permute-start.6 = (bf16[256,128]{1,0:T(8,128)(2,1)S(1)}, bf16[256,128]{1,0:T(8,128)(2,1)S(1)}, u32[]{:S(2)}, u32[]{:S(2)}) collective-permute-start(bf16[256,128]{1,0:T(8,128)(2,1)S(1)} %get-tuple-element.42), channel_id=1, source_target_pairs={{0,8},{2,10},{4,12},{6,14},{8,0},{10,2},{12,4},{14,6},{16,24},{18,... | collective-permute-start | bytes 196616 | tf_op jit(solution)/shard_map/to_owners/ppermute | solution.py:296
  24.4 5.5 %collective-permute-start.7 = (bf16[256,128]{1,0:T(8,128)(2,1)S(1)}, bf16[256,128]{1,0:T(8,128)(2,1)S(1)}, u32[]{:S(2)}, u32[]{:S(2)}) collective-permute-start(bf16[256,128]{1,0:T(8,128)(2,1)S(1)} %line_total.1.own_ref), channel_id=1, source_target_pairs={{0,32},{1,17},{2,34},{3,19},{4,36},{5,21},{6,38},{7,23},{8,40},{9,... | collective-permute-start | bytes 196616 | tf_op jit(solution)/shard_map/along_y/ppermute | solution.py:281
  25.8 4.3 %collective-permute-start.8 = (bf16[256,128]{1,0:T(8,128)(2,1)S(1)}, bf16[256,128]{1,0:T(8,128)(2,1)S(1)}, u32[]{:S(2)}, u32[]{:S(2)}) collective-permute-start(bf16[256,128]{1,0:T(8,128)(2,1)S(1)} %line_total.1.own_ref), channel_id=1, source_target_pairs={{0,48},{1,49},{2,50},{3,51},{4,52},{5,53},{6,54},{7,55},{8,56},{9,... | collective-permute-start | bytes 196616 | tf_op jit(solution)/shard_map/along_y/ppermute | solution.py:281
  27.6 4.6 %collective-permute-start.9 = (bf16[256,128]{1,0:T(8,128)(2,1)S(1)}, bf16[256,128]{1,0:T(8,128)(2,1)S(1)}, u32[]{:S(2)}, u32[]{:S(2)}) collective-permute-start(bf16[256,128]{1,0:T(8,128)(2,1)S(1)} %line_total.1.own_ref), channel_id=1, source_target_pairs={{0,16},{1,33},{2,18},{3,35},{4,20},{5,37},{6,22},{7,39},{8,24},{9,... | collective-permute-start | bytes 196616 | tf_op jit(solution)/shard_map/along_y/ppermute | solution.py:281
  32.6 4.1 %collective-permute-start.10 = (bf16[256,128]{1,0:T(8,128)(2,1)S(1)}, bf16[256,128]{1,0:T(8,128)(2,1)S(1)}, u32[]{:S(2)}, u32[]{:S(2)}) collective-permute-start(bf16[256,128]{1,0:T(8,128)(2,1)S(1)} %plane_total.1.own_ref), channel_id=1, source_target_pairs={{0,128},{1,65},{2,130},{3,67},{4,132},{5,69},{6,134},{7,71},{8,136... | collective-permute-start | bytes 196616 | tf_op jit(solution)/shard_map/along_x/ppermute | solution.py:281
  34.0 4.3 %collective-permute-start.11 = (bf16[256,128]{1,0:T(8,128)(2,1)S(1)}, bf16[256,128]{1,0:T(8,128)(2,1)S(1)}, u32[]{:S(2)}, u32[]{:S(2)}) collective-permute-start(bf16[256,128]{1,0:T(8,128)(2,1)S(1)} %plane_total.1.own_ref), channel_id=1, source_target_pairs={{0,192},{1,193},{2,194},{3,195},{4,196},{5,197},{6,198},{7,199},{8... | collective-permute-start | bytes 196616 | tf_op jit(solution)/shard_map/along_x/ppermute | solution.py:281
  35.7 4.6 %collective-permute-start.12 = (bf16[256,128]{1,0:T(8,128)(2,1)S(1)}, bf16[256,128]{1,0:T(8,128)(2,1)S(1)}, u32[]{:S(2)}, u32[]{:S(2)}) collective-permute-start(bf16[256,128]{1,0:T(8,128)(2,1)S(1)} %plane_total.1.own_ref), channel_id=1, source_target_pairs={{0,64},{1,129},{2,66},{3,131},{4,68},{5,133},{6,70},{7,135},{8,72}... | collective-permute-start | bytes 196616 | tf_op jit(solution)/shard_map/along_x/ppermute | solution.py:281
  40.3 16.1 %copy-start.2 = (bf16[2,8,128,128]{3,2,1,0:T(8,128)(2,1)S(1)}, bf16[2,8,128,128]{3,2,1,0:T(8,128)(2,1)}, u32[]{:S(2)}) copy-start(bf16[2,8,128,128]{3,2,1,0:T(8,128)(2,1)} %trans_ref.1) | copy-start | bytes 1572868
  40.3 16.1 %copy-start.3 = (bf16[128,1024]{1,0:T(8,128)(2,1)S(1)}, bf16[128,1024]{1,0:T(8,128)(2,1)}, u32[]{:S(2)}) copy-start(bf16[128,1024]{1,0:T(8,128)(2,1)} %query_ref.3) | copy-start | bytes 786436
  41.0 15.5 %copy-start = (bf16[128,1024]{1,0:T(8,128)(2,1)S(1)}, bf16[128,1024]{1,0:T(8,128)(2,1)}, u32[]{:S(2)}) copy-start(bf16[128,1024]{1,0:T(8,128)(2,1)} %key_ref.3) | copy-start | bytes 786436
  41.0 15.5 %copy-start.1 = (bf16[128,1024]{1,0:T(8,128)(2,1)S(1)}, bf16[128,1024]{1,0:T(8,128)(2,1)}, u32[]{:S(2)}) copy-start(bf16[128,1024]{1,0:T(8,128)(2,1)} %value_ref.3) | copy-start | bytes 786436
  57.2 5.3 %collective-permute-start.13 = (bf16[64,1024]{1,0:T(8,128)(2,1)S(1)}, bf16[64,1024]{1,0:T(8,128)(2,1)S(1)}, u32[]{:S(2)}, u32[]{:S(2)}) collective-permute-start(bf16[64,1024]{1,0:T(8,128)(2,1)S(1)} %get-tuple-element.64), channel_id=1, source_target_pairs={{0,1},{1,0},{2,3},{3,2},{4,5},{5,4},{6,7},{7,6},{8,9},{9,8},{10,11... | collective-permute-start | bytes 393224 | tf_op jit(solution)/shard_map/to_tokens/ppermute | solution.py:326
